TPU v7x, 512 devices: a whole 4x4x16 slice. The times are simulated.
512 devices in a mesh: row: 64 (over x, z), col: 8 (over y, core).
Axes of the slice: x: 4, y: 4, z: 16, core: 2. Of those that a mesh axis runs over, the one named last changes fastest.
Arguments:
- slab_rows: float32 [131072, 1024], P('row', 'col')
- row_flips: int32 [131072], P('row'), may hold values from 0 to 1
- sample_holder: int32 [8192, 1], P('row'), may hold values from 0 to 63; in each aligned block of 128 rows (0 to 127, 128 to 255, ...) at most 4 rows name the same one
- sample_offset: int32 [8192], P('row'), may hold values from 0 to 2047
Outputs:
- mixed_slab: float32 [131072, 1024], P('row', 'col')
- precond: float32 [1024, 1024], P(None, 'col')
Inputs may be any that keep to these rules, and one draw needn't show every extreme that they name: `sample_holder`: each owner's list of 128 entries names no holder more than 4 times, and in every draw some list names one holder exactly 4 times.
All inputs are finite; a program needn't handle non-finite values.
Results may differ from a plain program's by a relative error of at most 0.0003.
Values sent between devices are 32-bit elements; how exact they have to be, the bound alone decides.
A program may use at most 64 MiB of HBM per device.

v0:
```python
import math

import jax
import jax.numpy as jnp
from jax import lax
from jax.sharding import PartitionSpec as P

PRECISE = lax.Precision.HIGHEST


def from_partner(array, axis, apart):
    return lax.ppermute(array, axis, [(i, i ^ 1 << apart) for i in range(lax.axis_size(axis))])


def hadamard(table_size):
    indices = jnp.arange(table_size, dtype=jnp.int32)
    shared = indices[:, None] & indices[None, :]
    parity = jnp.zeros((table_size, table_size), jnp.int32)
    for bit_pos in range(max(table_size.bit_length() - 1, 0)):
        parity = parity ^ shared >> bit_pos & 1
    return (1 - 2 * parity).astype(jnp.float32)


def per_device(slab_rows, row_flips, sample_holder, sample_offset):
    local_rows = slab_rows.shape[0]
    width_local = slab_rows.shape[1]
    groups = lax.axis_size("row")
    position = lax.axis_index("row")
    inner = min(local_rows, 128)
    outer = local_rows // inner
    signs = (1 - 2 * row_flips).astype(jnp.float32)
    signed = slab_rows * signs[:, None]
    blocks = signed.reshape(outer, inner, width_local)
    blocks = jnp.einsum("pb,abc->apc", hadamard(inner), blocks, precision=PRECISE)
    blocks = jnp.einsum("qa,apc->qpc", hadamard(outer), blocks, precision=PRECISE)
    values = blocks.reshape(local_rows, width_local)
    for section_bit in range(groups.bit_length() - 1):
        partner = from_partner(values, "row", section_bit)
        upper_half = position >> section_bit & 1 == 1
        values = jnp.where(upper_half, partner - values, values + partner)
    mixed_slab = values * (1.0 / math.sqrt(local_rows * groups))
    holders_all, offsets_all = (
        lax.all_gather(sample_holder[:, 0], "row", axis=0, tiled=True),
        lax.all_gather(sample_offset, "row", axis=0, tiled=True),
    )
    samples = holders_all.shape[0]
    per_owner = sample_offset.shape[0]
    capacity = 2 * per_owner // groups
    total_slots = groups * capacity
    mine = holders_all == position
    mine_grid = mine.reshape(groups, per_owner)
    rank = jnp.cumsum(mine_grid.astype(jnp.int32), axis=1) - 1
    owners = jnp.arange(groups, dtype=jnp.int32)[:, None]
    slot = jnp.where(mine_grid, owners * capacity + rank, total_slots).reshape(samples)
    source = jnp.zeros((total_slots,), jnp.int32).at[slot].set(offsets_all, mode="drop")
    filled = jnp.zeros((total_slots,), jnp.float32).at[slot].set(1.0, mode="drop")
    packed = jnp.take(mixed_slab, source, axis=0) * filled[:, None]
    arrived = lax.all_to_all(
        packed.reshape(groups, capacity, width_local),
        "row",
        split_axis=0,
        concat_axis=0,
        tiled=True,
    )
    packed = arrived.reshape(total_slots, width_local)
    partial_block = jnp.einsum(
        "sk,sc->kc", lax.all_gather(packed, "col", axis=1, tiled=True), packed, precision=PRECISE
    )
    gram_block = lax.psum(partial_block, "row")
    gram = lax.all_gather(gram_block, "col", axis=1, tiled=True)
    lower = jnp.linalg.cholesky(gram * (1.0 / samples))
    upper = lower.T
    precond = lax.dynamic_slice_in_dim(upper, lax.axis_index("col") * width_local, width_local, 1)
    return (mixed_slab, precond)


def solution(mesh):
    in_specs = (P("row", "col"), P("row"), P("row", None), P("row"))
    out_specs = (P("row", "col"), P(None, "col"))
    return jax.shard_map(
        per_device, mesh=mesh, in_specs=in_specs, out_specs=out_specs, check_vma=False
    )
```

profile of v0, /device:TPU:1, one launch (start us, length us, event | category | flops | bytes accessed | tf_op | source)
XLA Modules:
  0.0 1137.4 jit_solution(3040349270031435559)
XLA Ops:
  7.9 1.6 broadcast_multiply_fusion.1
  9.5 1.8 convolution_bitcast_fusion
  13.2 4.4 collective-permute-start
  17.6 18.3 %collective-permute-done = f32[2048,128]{1,0:T(8,128)S(1)} collective-permute-done((f32[2048,128]{1,0:T(8,128)S(1)}, f32[2048,128]{1,0:T(8,128)S(1)}, u32[]{:S(2)}, u32[]{:S(2)}) %collective-permute-start) | collective-permute-done | bytes 1048608 | tf_op jit(solution)/shard_map/ppermute | solution.py:12
  35.9 9.4 collective-permute-start.1
  45.3 45.0 %collective-permute-done.1 = f32[2048,128]{1,0:T(8,128)S(1)} collective-permute-done((f32[2048,128]{1,0:T(8,128)S(1)}, f32[2048,128]{1,0:T(8,128)S(1)}, u32[]{:S(2)}, u32[]{:S(2)}) %collective-permute-start.1) | collective-permute-done | bytes 1048608 | tf_op jit(solution)/shard_map/ppermute | solution.py:12
  90.5 8.8 collective-permute-start.2
  99.3 112.7 %collective-permute-done.2 = f32[2048,128]{1,0:T(8,128)S(1)} collective-permute-done((f32[2048,128]{1,0:T(8,128)S(1)}, f32[2048,128]{1,0:T(8,128)S(1)}, u32[]{:S(2)}, u32[]{:S(2)}) %collective-permute-start.2) | collective-permute-done | bytes 1048608 | tf_op jit(solution)/shard_map/ppermute | solution.py:12
  212.1 57.9 %collective-permute-start.3 = (f32[2048,128]{1,0:T(8,128)S(1)}, f32[2048,128]{1,0:T(8,128)S(1)}, u32[]{:S(2)}, u32[]{:S(2)}) collective-permute-start(f32[2048,128]{1,0:T(8,128)S(1)} %add_select_fusion.2), channel_id=1, source_target_pairs={{0,64},{8,72},{16,80},{24,88},{32,96},{40,104},{48,112},{56,120},{... | collective-permute-start | bytes 3145736 | tf_op jit(solution)/shard_map/ppermute | solution.py:12
  270.1 45.5 %collective-permute-done.3 = f32[2048,128]{1,0:T(8,128)S(1)} collective-permute-done((f32[2048,128]{1,0:T(8,128)S(1)}, f32[2048,128]{1,0:T(8,128)S(1)}, u32[]{:S(2)}, u32[]{:S(2)}) %collective-permute-start.3) | collective-permute-done | bytes 1048608 | tf_op jit(solution)/shard_map/ppermute | solution.py:12
  315.7 3.1 collective-permute-start.4
  318.8 71.7 %all-gather = s32[8192,1]{0,1:T(1,128)S(1)} all-gather(s32[128,1]{0,1:T(1,128)S(1)} %copy-done.2), channel_id=2, replica_groups=mesh['row'=64,'col'=8] {'row'}, dimensions={0}, use_global_device_ids=true | all-gather | bytes 33280 | tf_op jit(solution)/shard_map/all_gather | solution.py:43
  390.8 3.4 collective-permute-start.5
  394.5 63.3 %all-gather.1 = s32[64,1,128]{2,1,0:T(1,128)S(1)} all-gather(s32[1,1,128]{2,1,0:T(1,128)S(1)} %bitcast.77), channel_id=1, replica_groups=mesh['row'=64,'col'=8] {'row'}, dimensions={0}, use_global_device_ids=true | all-gather | bytes 33280 | tf_op jit(solution)/shard_map/all_gather | solution.py:44
  457.9 30.4 %scatter_custom_fusion = s32[256]{0:T(256)S(1)} fusion(s32[8192]{0:T(1024)S(1)} %compare_select_fusion, s32[8192]{0:T(1024)S(1)} %bitcast.76, s32[]{:T(128)} %constant.317.clone.1), kind=kCustom, calls=%fused_computation.160 | custom fusion | bytes 1028 | tf_op jit(solution)/shard_map/scatter | solution.py:55
  488.4 30.4 %scatter_custom_fusion.1 = f32[256]{0:T(256)S(1)} fusion(s32[8192]{0:T(1024)S(1)} %compare_select_fusion, f32[8192]{0:T(1024)S(1)} %broadcast.376, f32[]{:T(128)} %constant.325.clone.1), kind=kCustom, calls=%fused_computation.157 | custom fusion | bytes 1028 | tf_op jit(solution)/shard_map/scatter | solution.py:56
  520.1 22.2 %all_to_all.5 = f32[64,4,128]{2,1,0:T(4,128)} all-to-all(f32[64,4,128]{2,1,0:T(4,128)S(1)} %select_multiply_fusion.1), channel_id=1, replica_groups=mesh['row'=64,'col'=8] {'row'}, dimensions={0} | all-to-all | bytes 262144 | tf_op jit(solution)/shard_map/all_to_all | solution.py:58
  542.4 58.6 %all-gather.5.cloned.1.call-done = f32[256,1024]{1,0:T(8,128)} async-done(((f32[256,128]{1,0:T(8,128)}), f32[256,1024]{1,0:T(8,128)}) %all-gather.5.cloned.1.call-update) | async-done | bytes 1048592 | tf_op jit(solution)/shard_map/all_gather | solution.py:67
  601.0 2.8 fusion.102
  603.8 257.7 %all-reduce.3.cloned.1.call-done = f32[1024,128]{0,1:T(8,128)} async-done(((f32[1024,128]{0,1:T(8,128)}), f32[1024,128]{0,1:T(8,128)}) %all-reduce.3.cloned.1.call-update) | async-done | bytes 524304 | tf_op jit(solution)/shard_map/psum | solution.py:69
  861.5 47.1 %all-gather.7.cloned.1.call-done = f32[1024,1024]{0,1:T(8,128)} async-done(((f32[1024,128]{0,1:T(8,128)}), f32[1024,1024]{0,1:T(8,128)}) %all-gather.7.cloned.1.call-update) | async-done | bytes 4194320 | tf_op jit(solution)/shard_map/all_gather | solution.py:70
  908.6 5.0 broadcast_multiply_fusion
  913.6 5.8 copy.17
  919.4 4.4 fusion
  923.8 1.9 copy-done
  925.8 11.7 %cholesky.223 = f32[128,128]{1,0:T(8,128)S(1)} custom-call(f32[128,128]{1,0:T(8,128)S(1)} %cholesky.580), custom_call_target="Cholesky" | custom-call | tf_op jit(solution)/shard_map/jit(cholesky)/cholesky | solution.py:71
  937.5 2.5 cholesky.255
  940.0 9.8 custom-call.59
  949.8 2.4 constant_dynamic-update-slice_fusion.6
  953.8 11.9 %cholesky.244 = f32[128,128]{1,0:T(8,128)S(1)} custom-call(f32[128,128]{1,0:T(8,128)S(1)} %cholesky.584), custom_call_target="Cholesky" | custom-call | tf_op jit(solution)/shard_map/jit(cholesky)/cholesky | solution.py:71
  966.3 9.8 custom-call.60
  977.3 2.1 convolution_subtract_fusion.1
  979.4 11.7 %cholesky.468 = f32[128,128]{1,0:T(8,128)S(1)} custom-call(f32[128,128]{1,0:T(8,128)S(1)} %cholesky.589), custom_call_target="Cholesky" | custom-call | tf_op jit(solution)/shard_map/jit(cholesky)/cholesky | solution.py:71
  992.4 9.8 custom-call.61
  1003.4 2.3 convolution_subtract_fusion.2
  1005.7 11.9 %cholesky.487 = f32[128,128]{1,0:T(8,128)S(1)} custom-call(f32[128,128]{1,0:T(8,128)S(1)} %cholesky.594), custom_call_target="Cholesky" | custom-call | tf_op jit(solution)/shard_map/jit(cholesky)/cholesky | solution.py:71
  1018.9 9.8 custom-call.62
  1029.9 2.3 convolution_subtract_fusion.3
  1032.2 11.7 %cholesky.506 = f32[128,128]{1,0:T(8,128)S(1)} custom-call(f32[128,128]{1,0:T(8,128)S(1)} %cholesky.599), custom_call_target="Cholesky" | custom-call | tf_op jit(solution)/shard_map/jit(cholesky)/cholesky | solution.py:71
  1045.2 10.2 custom-call.63
  1056.4 2.3 convolution_subtract_fusion.4
  1058.7 11.7 %cholesky.526 = f32[128,128]{1,0:T(8,128)S(1)} custom-call(f32[128,128]{1,0:T(8,128)S(1)} %cholesky.604), custom_call_target="Cholesky" | custom-call | tf_op jit(solution)/shard_map/jit(cholesky)/cholesky | solution.py:71
  1071.7 9.8 custom-call.64
  1082.5 2.0 convolution_subtract_fusion.5
  1084.5 11.9 %cholesky.546 = f32[128,128]{1,0:T(8,128)S(1)} custom-call(f32[128,128]{1,0:T(8,128)S(1)} %cholesky.609), custom_call_target="Cholesky" | custom-call | tf_op jit(solution)/shard_map/jit(cholesky)/cholesky | solution.py:71
  1097.6 9.8 custom-call.65
  1108.3 1.8 convolution_subtract_fusion.6
  1110.1 11.7 %cholesky.564 = f32[128,128]{1,0:T(8,128)S(1)} custom-call(f32[128,128]{1,0:T(8,128)S(1)} %convolution_subtract_fusion.6), custom_call_target="Cholesky" | custom-call | tf_op jit(solution)/shard_map/jit(cholesky)/cholesky | solution.py:71
  (69 shorter events, 24.2 us)
Async XLA Ops:
  7.2 593.8 %all-gather.5.cloned.1.call-start = ((), (), s32[]{:S(2)}) async-start(), calls=%async_computation.1 | async-start | bytes 1179648 | tf_op jit(solution)/shard_map/all_gather | solution.py:67
  13.2 22.7 %collective-permute-start = (f32[2048,128]{1,0:T(8,128)S(1)}, f32[2048,128]{1,0:T(8,128)S(1)}, u32[]{:S(2)}, u32[]{:S(2)}) collective-permute-start(f32[2048,128]{1,0:T(8,128)S(1)} %bitcast.71), channel_id=1, source_target_pairs={{0,8},{8,0},{16,24},{24,16},{32,40},{40,32},{48,56},{56,48},{64,72... | collective-permute-start | bytes 3145736 | tf_op jit(solution)/shard_map/ppermute | solution.py:12
  35.9 54.4 %collective-permute-start.1 = (f32[2048,128]{1,0:T(8,128)S(1)}, f32[2048,128]{1,0:T(8,128)S(1)}, u32[]{:S(2)}, u32[]{:S(2)}) collective-permute-start(f32[2048,128]{1,0:T(8,128)S(1)} %add_select_fusion.4), channel_id=1, source_target_pairs={{0,16},{8,24},{16,0},{24,8},{32,48},{40,56},{48,32},{56,40},{64,80... | collective-permute-start | bytes 3145736 | tf_op jit(solution)/shard_map/ppermute | solution.py:12
  45.3 273.5 %copy-start.2 = (s32[128,1]{0,1:T(1,128)S(1)}, s32[128,1]{0,1:T(1,128)}, u32[]{:S(2)}) copy-start(s32[128,1]{0,1:T(1,128)} %param.6) | copy-start | bytes 1540
  90.5 121.5 %collective-permute-start.2 = (f32[2048,128]{1,0:T(8,128)S(1)}, f32[2048,128]{1,0:T(8,128)S(1)}, u32[]{:S(2)}, u32[]{:S(2)}) collective-permute-start(f32[2048,128]{1,0:T(8,128)S(1)} %add_select_fusion.3), channel_id=1, source_target_pairs={{0,32},{8,40},{16,48},{24,56},{32,0},{40,8},{48,16},{56,24},{64,96... | collective-permute-start | bytes 3145736 | tf_op jit(solution)/shard_map/ppermute | solution.py:12
  99.3 295.2 %copy-start.3 = (s32[128]{0:T(128)S(1)}, s32[128]{0:T(128)}, u32[]{:S(2)}) copy-start(s32[128]{0:T(128)} %param.7) | copy-start | bytes 1540
  212.1 103.4 %collective-permute-start.3 = (f32[2048,128]{1,0:T(8,128)S(1)}, f32[2048,128]{1,0:T(8,128)S(1)}, u32[]{:S(2)}, u32[]{:S(2)}) collective-permute-start(f32[2048,128]{1,0:T(8,128)S(1)} %add_select_fusion.2), channel_id=1, source_target_pairs={{0,64},{8,72},{16,80},{24,88},{32,96},{40,104},{48,112},{56,120},{... | collective-permute-start | bytes 3145736 | tf_op jit(solution)/shard_map/ppermute | solution.py:12
  315.7 75.0 %collective-permute-start.4 = (f32[2048,128]{1,0:T(8,128)S(1)}, f32[2048,128]{1,0:T(8,128)S(1)}, u32[]{:S(2)}, u32[]{:S(2)}) collective-permute-start(f32[2048,128]{1,0:T(8,128)S(1)} %add_select_fusion.1), channel_id=1, source_target_pairs={{0,128},{8,136},{16,144},{24,152},{32,160},{40,168},{48,176},{56,1... | collective-permute-start | bytes 3145736 | tf_op jit(solution)/shard_map/ppermute | solution.py:12
  390.8 128.2 %collective-permute-start.5 = (f32[2048,128]{1,0:T(8,128)S(1)}, f32[2048,128]{1,0:T(8,128)S(1)}, u32[]{:S(2)}, u32[]{:S(2)}) collective-permute-start(f32[2048,128]{1,0:T(8,128)S(1)} %add_select_fusion), channel_id=1, source_target_pairs={{0,256},{8,264},{16,272},{24,280},{32,288},{40,296},{48,304},{56,3... | collective-permute-start | bytes 3145736 | tf_op jit(solution)/shard_map/ppermute | solution.py:12
  519.2 394.4 %copy-start.1 = (f32[2048,128]{1,0:T(8,128)}, f32[2048,128]{1,0:T(8,128)S(1)}, u32[]{:S(2)}) copy-start(f32[2048,128]{1,0:T(8,128)S(1)} %select_multiply_fusion) | copy-start | bytes 3145732
  542.3 319.2 %all-reduce.3.cloned.1.call-start = ((), (), s32[]{:S(2)}) async-start(), calls=%async_computation.2 | async-start | bytes 1048576 | tf_op jit(solution)/shard_map/psum | solution.py:69
  603.8 304.8 %all-gather.7.cloned.1.call-start = ((), (), s32[]{:S(2)}) async-start(), calls=%async_computation.3 | async-start | bytes 4718592 | tf_op jit(solution)/shard_map/all_gather | solution.py:70
  923.8 1.9 copy-start
Sparse Core Ops, SparseCore 0:
  542.4 58.5 all-gather.4
  605.0 256.4 all-reduce.2
  863.9 44.6 all-gather.6
where the time goes:
time: 1150 us; the launch traced here: 1140 us
  waiting for transfers between devices  585 us (51%)
  other arithmetic  186 us (16%)
  blocking collectives  157 us (14%)
  starting transfers between devices  87.2 us (8%)
  local copies, waits for them, and re-layouts  73.9 us (6%)
  matrix products  28.6 us (2%)
  between operations  19.2 us (2%)
    psum x1, waiting for transfers between devices, per_device(): gram_block = lax.psum(partial_block, 'row')  258 us
    ppermute x6, waiting for transfers between devices, from_partner(): lax.ppermute(array, axis, [(i, i ^ 1 << apart) for i in range(lax.axis_si...  221 us
    another operation x30, other arithmetic, per_device(): lower = jnp.linalg.cholesky(gram * (1.0 / samples))  172 us
    ppermute x6, starting transfers between devices, from_partner(): lax.ppermute(array, axis, [(i, i ^ 1 << apart) for i in range(lax.axis_si...  87 us
    all_gather x1, blocking collectives, per_device(): lax.all_gather(sample_holder[:, 0], 'row', axis=0, tiled=True)  71.7 us
    all_gather x1, blocking collectives, per_device(): lax.all_gather(sample_offset, 'row', axis=0, tiled=True)  63.3 us
    all_gather x1, waiting for transfers between devices, per_device(): lax.all_gather(packed, 'col', axis=1, tiled=True)  58.6 us
    all_gather x1, waiting for transfers between devices, per_device(): gram = lax.all_gather(gram_block, 'col', axis=1, tiled=True)  47.1 us
  transfers between devices with their start and end apart: 9, of which 7 were waited for; matrix products, arithmetic and copies ran while one was open for 5% of the time, Pallas kernels for 0%

commit v1 on v0

v1 whole, which is shorter than its diff:
```python
import functools
import math

import jax
import jax.numpy as jnp
from jax import lax
from jax.experimental import pallas as pl
from jax.experimental.pallas import tpu as pltpu
from jax.sharding import PartitionSpec as P

MESH = pl.DeviceIdType.MESH
PRECISE = lax.Precision.HIGHEST
F32, BF16 = jnp.float32, jnp.bfloat16
TILE = 128


def split_three(values):
    high = values.astype(BF16)
    rest = values - high.astype(F32)
    middle = rest.astype(BF16)
    return high, middle, (rest - middle.astype(F32)).astype(BF16)


def exact_dot(left, values):
    return sum(jnp.dot(left, part, preferred_element_type=F32) for part in split_three(values))


def butterfly(items):
    items, apart = list(items), 1
    while apart < len(items):
        for i in range(len(items)):
            if not i & apart:
                items[i], items[i + apart] = items[i] + items[i + apart], items[i] - items[i + apart]
        apart *= 2
    return items


def wait_for(ref, sem):
    pltpu.make_async_copy(ref, ref, sem).wait()


def mix_kernel(nx, nz, scale, x_ref, sign_ref, key_ref, out_ref, keys_ref, work, recv, back, send_sem, recv_sem):
    n = nx * nz
    blocks, chunk = sign_ref.shape[0], work.shape[1]
    per_block = TILE // chunk
    me, col = lax.axis_index("row"), lax.axis_index("col")
    mx, mz = lax.div(me, nz), lax.rem(me, nz)

    def peer(k):
        dx, m = lax.rem(k, nx), lax.div(k, nx)
        dz = nz + lax.div(m + 1, 2) * (2 * lax.rem(m, 2) - 1)
        return lax.rem(mx + dx, nx) * nz + lax.rem(mz + dz, nz)

    barrier = pltpu.get_barrier_semaphore()

    def greet(k, carry):
        pl.semaphore_signal(barrier, inc=1, device_id=(peer(k), col), device_id_type=MESH)
        return carry

    lax.fori_loop(1, n, greet, 0)

    shared = lax.broadcasted_iota(jnp.int32, (TILE, TILE), 0) & lax.broadcasted_iota(jnp.int32, (TILE, TILE), 1)
    shared = shared ^ shared >> 4
    shared = shared ^ shared >> 2
    shared = shared ^ shared >> 1
    table = (1 - 2 * (shared & 1)).astype(F32)

    def inner(a, carry):
        left = (table * sign_ref[pl.ds(a, 1), :]).astype(BF16)
        rows = x_ref[pl.ds(pl.multiple_of(a * TILE, TILE), TILE), :]
        work[pl.ds(a * per_block, per_block)] = exact_dot(left, rows).reshape(per_block, chunk, TILE)
        return carry

    lax.fori_loop(0, blocks, inner, 0)

    def outer(b, carry):
        part, at = lax.div(b * 8, chunk), pl.multiple_of(lax.rem(b * 8, chunk), 8)
        mixed = butterfly([work[a * per_block + part, pl.ds(at, 8), :] for a in range(blocks)])
        for a in range(blocks):
            work[a * per_block + part, pl.ds(at, 8), :] = mixed[a]
        return carry

    lax.fori_loop(0, TILE // 8, outer, 0)
    pl.semaphore_wait(barrier, n - 1)

    def send(src, dst, device, which):
        pltpu.make_async_remote_copy(
            src_ref=src, dst_ref=dst, send_sem=send_sem.at[which], recv_sem=recv_sem.at[which],
            device_id=(device, col), device_id_type=MESH,
        ).start()

    def there(k, carry):
        device = peer(k)
        send(key_ref, keys_ref.at[me], device, 0)
        send(work.at[device], recv.at[me], device, 1)
        return carry

    lax.fori_loop(1, n, there, 0)
    keys_ref[me] = key_ref[...]
    recv[me] = work[me]
    wait_for(recv.at[pl.ds(0, n - 1)], recv_sem.at[1])

    def low(g, carry):
        mixed = butterfly([recv[8 * g + i] for i in range(8)])
        for i in range(8):
            recv[8 * g + i] = mixed[i]
        return carry

    def high(i, carry):
        mixed = butterfly([recv[8 * g + i] for g in range(n // 8)])
        for g in range(n // 8):
            back[8 * g + i] = mixed[g] * scale
        return carry

    lax.fori_loop(0, n // 8, low, 0)
    lax.fori_loop(0, 8, high, 0)

    def home(k, carry):
        device = peer(k)
        send(back.at[device], out_ref.at[me], device, 2)
        return carry

    lax.fori_loop(1, n, home, 0)
    out_ref[me] = back[me]
    wait_for(keys_ref.at[pl.ds(0, n - 1)], recv_sem.at[0])
    wait_for(out_ref.at[pl.ds(0, n - 1)], recv_sem.at[2])
    wait_for(keys_ref.at[pl.ds(0, n - 1)], send_sem.at[0])
    wait_for(recv.at[pl.ds(0, n - 1)], send_sem.at[1])
    wait_for(out_ref.at[pl.ds(0, n - 1)], send_sem.at[2])


def gram_kernel(nx, nz, nc, local, mixed_ref, keys_ref, gram_ref, packed, part, arrived, middle, pieces, send_sem, recv_sem):
    n, owners = nx * nz, keys_ref.shape[0]
    slots = packed.shape[1]
    capacity = slots // owners
    samples = owners * keys_ref.shape[1]
    rows_x = part.shape[2]
    me, mc = lax.axis_index("row"), lax.axis_index("col")
    mx, mz = lax.div(me, nz), lax.rem(me, nz)

    def along_col(d):
        return me, lax.rem(mc + d, nc)

    def along_x(d):
        return lax.rem(mx + d, nx) * nz + mz, mc

    def along_z(d):
        return mx * nz + lax.rem(mz + d, nz), mc

    barrier = pltpu.get_barrier_semaphore()
    for count, peer in ((nc, along_col), (nx, along_x), (nz, along_z)):
        for d in range(1, count):
            pl.semaphore_signal(barrier, inc=1, device_id=peer(d), device_id_type=MESH)

    holder, offset = keys_ref[...] // local, keys_ref[...] % local
    mine = jnp.where(holder == me, 1.0, 0.0)
    before = lax.broadcasted_iota(jnp.int32, (TILE, TILE), 0) < lax.broadcasted_iota(jnp.int32, (TILE, TILE), 1)
    rank = jnp.dot(mine.astype(BF16), jnp.where(before, 1.0, 0.0).astype(BF16), preferred_element_type=F32)
    wanted = []
    for q in range(capacity):
        chosen = jnp.where(rank == q, mine, 0.0)
        row = jnp.sum(chosen * (offset + 1).astype(F32), axis=1, keepdims=True) - 1.0
        wanted.append(jnp.broadcast_to(row, (owners, TILE)))
    wanted = jnp.concatenate(wanted, axis=0).astype(jnp.int32)
    lanes = lax.broadcasted_iota(jnp.int32, (slots, TILE), 1)

    def pick(a, total):
        chosen = jnp.where(wanted == lanes + a * TILE, 1.0, 0.0).astype(BF16)
        return total + exact_dot(chosen, mixed_ref[pl.ds(pl.multiple_of(a * TILE, TILE), TILE), :])

    packed[mc] = lax.fori_loop(0, local // TILE, pick, jnp.zeros((slots, TILE), F32))
    pl.semaphore_wait(barrier, nc + nx + nz - 3)

    def send(src, dst, device, which):
        pltpu.make_async_remote_copy(
            src_ref=src, dst_ref=dst, send_sem=send_sem.at[which], recv_sem=recv_sem.at[which],
            device_id=device, device_id_type=MESH,
        ).start()

    for d in range(1, nc):
        send(packed.at[mc], packed.at[mc], along_col(d), 0)
    wait_for(packed.at[pl.ds(0, nc - 1)], recv_sem.at[0])
    mine_packed = packed[mc]

    def multiply(b, carry):
        block = lax.dot_general(packed[b], mine_packed, (((0,), (0,)), ((), ())), precision=PRECISE, preferred_element_type=F32)
        for q in range(nx):
            part[q, b] = block[q * rows_x:(q + 1) * rows_x]
        return carry

    lax.fori_loop(0, nc, multiply, 0)
    for d in range(1, nx):
        send(part.at[lax.rem(mx + d, nx)], arrived.at[mx], along_x(d), 1)
    arrived[mx] = part[mx]
    wait_for(arrived.at[pl.ds(0, nx - 1)], recv_sem.at[1])
    total = arrived[0]
    for q in range(1, nx):
        total = total + arrived[q]
    middle[...] = total.reshape(middle.shape)
    for d in range(1, nz):
        send(middle.at[lax.rem(mz + d, nz)], pieces.at[mz], along_z(d), 2)
    pieces[mz] = middle[mz]
    wait_for(pieces.at[pl.ds(0, nz - 1)], recv_sem.at[2])
    total = pieces[0]
    for q in range(1, nz):
        total = total + pieces[q]
    gram_ref[mc, mx, mz] = total * (1.0 / samples)

    own = gram_ref.at[mc, mx, mz]
    for d in range(1, nz):
        send(own, own, along_z(d), 3)
    wait_for(gram_ref.at[mc, mx, pl.ds(0, nz - 1)], recv_sem.at[3])
    own = gram_ref.at[mc, mx]
    for d in range(1, nx):
        send(own, own, along_x(d), 4)
    wait_for(gram_ref.at[mc, pl.ds(0, nx - 1)], recv_sem.at[4])
    own = gram_ref.at[mc]
    for d in range(1, nc):
        send(own, own, along_col(d), 5)
    wait_for(gram_ref.at[pl.ds(0, nc - 1)], recv_sem.at[5])

    wait_for(packed.at[pl.ds(0, nc - 1)], send_sem.at[0])
    wait_for(arrived.at[pl.ds(0, nx - 1)], send_sem.at[1])
    wait_for(pieces.at[pl.ds(0, nz - 1)], send_sem.at[2])
    wait_for(gram_ref.at[mc, mx, pl.ds(0, nz - 1)], send_sem.at[3])
    wait_for(gram_ref.at[mc, pl.ds(0, nx - 1)], send_sem.at[4])
    wait_for(gram_ref.at[pl.ds(0, nc - 1)], send_sem.at[5])


def params(number):
    return pltpu.CompilerParams(collective_id=number, has_side_effects=True, vmem_limit_bytes=40 * 2**20)


def per_device(nx, nz, nc, slab_rows, row_flips, sample_holder, sample_offset):
    local, width = slab_rows.shape
    n = nx * nz
    per_owner = sample_offset.shape[0]
    chunk = local // n
    vmem = pl.BlockSpec(memory_space=pltpu.VMEM)
    signs = (1 - 2 * row_flips).astype(F32).reshape(local // TILE, TILE)
    key = (sample_holder[:, 0] * local + sample_offset).reshape(1, per_owner)
    mixed, keys = pl.pallas_call(
        functools.partial(mix_kernel, nx, nz, 1.0 / math.sqrt(local * n)),
        out_shape=(
            jax.ShapeDtypeStruct((n, chunk, width), F32),
            jax.ShapeDtypeStruct((n, 1, per_owner), jnp.int32),
        ),
        in_specs=[vmem] * 3,
        out_specs=(vmem, vmem),
        scratch_shapes=[pltpu.VMEM((n, chunk, width), F32)] * 3
        + [pltpu.SemaphoreType.DMA((3,)), pltpu.SemaphoreType.DMA((3,))],
        compiler_params=params(0),
        name="mix",
    )(slab_rows, signs, key)
    mixed_slab = mixed.reshape(local, width)
    capacity = 2 * per_owner // n
    rows_x, rows_z = TILE // nx, TILE * nc // (nx * nz)
    gram = pl.pallas_call(
        functools.partial(gram_kernel, nx, nz, nc, local),
        out_shape=jax.ShapeDtypeStruct((nc, nx, nz, rows_z, TILE), F32),
        in_specs=[vmem] * 2,
        out_specs=vmem,
        scratch_shapes=[
            pltpu.VMEM((nc, n * capacity, width), F32),
            pltpu.VMEM((nx, nc, rows_x, TILE), F32),
            pltpu.VMEM((nx, nc, rows_x, TILE), F32),
            pltpu.VMEM((nz, rows_z, TILE), F32),
            pltpu.VMEM((nz, rows_z, TILE), F32),
            pltpu.SemaphoreType.DMA((6,)),
            pltpu.SemaphoreType.DMA((6,)),
        ],
        compiler_params=params(1),
        name="gram",
    )(mixed_slab, keys.reshape(n, per_owner))
    gram = gram.reshape(nc, nx, nc, nz // nc, rows_z, TILE).transpose(2, 1, 3, 4, 0, 5).reshape(nc * TILE, nc * TILE)
    upper = jnp.linalg.cholesky(gram).T
    precond = lax.dynamic_slice_in_dim(upper, lax.axis_index("col") * width, width, 1)
    return (mixed_slab, precond)


def solution(mesh):
    nx = 4
    nz = mesh.shape["row"] // nx
    in_specs = (P("row", "col"), P("row"), P("row", None), P("row"))
    out_specs = (P("row", "col"), P(None, "col"))
    return jax.shard_map(
        functools.partial(per_device, nx, nz, mesh.shape["col"]),
        mesh=mesh, in_specs=in_specs, out_specs=out_specs, check_vma=False,
    )
```

time: 1150 us -> 456 us (0.40)
  waiting for transfers between devices: 585 us -> 0 us
  Pallas kernels: 0 us -> 221 us
  blocking collectives: 157 us -> 0 us
  starting transfers between devices: 87.2 us -> 0 us
  local copies, waits for them, and re-layouts: 73.9 us -> 20.3 us
  between operations: 19.2 us -> 6.51 us
    psum x1 -> x0, waiting for transfers between devices: 258 us -> none  [per_device(): gram_block = lax.psum(partial_block, 'row')]
    ppermute x6 -> x0, waiting for transfers between devices: 221 us -> none  [from_partner(): lax.ppermute(array, axis, [(i, i ^ 1 << apart) for i in range(lax.axis_si...]
    pallas_call x0 -> x2, Pallas kernels: none -> 221 us  [the longest x1 117 us: per_device(): pl.pallas_call(functools.partial(mix_kernel, nx, nz, 1.0 / math.sqrt(loca...]
    all_gather x2 -> x0, blocking collectives: 135 us -> none  [the longest x1 71.7 us: per_device(): lax.all_gather(sample_holder[:, 0], 'row', axis=0, tiled=True)]
    all_gather x2 -> x0, waiting for transfers between devices: 106 us -> none  [the longest x1 58.6 us: per_device(): lax.all_gather(packed, 'col', axis=1, tiled=True)]
    ppermute x6 -> x0, starting transfers between devices: 87 us -> none  [from_partner(): lax.ppermute(array, axis, [(i, i ^ 1 << apart) for i in range(lax.axis_si...]
    scatter x2 -> x0, local copies, waits for them, and re-layouts: 60.9 us -> none  [the longest x1 30.4 us: per_device(): jnp.zeros((total_slots,), jnp.float32).at[slot].set(1.0, mode='drop')]
    all_to_all x1 -> x0, blocking collectives: 22.2 us -> none  [per_device(): lax.all_to_all(packed.reshape(groups, capacity, width_local), 'row', spli...]
  transfers between devices with their start and end apart: 9 -> 0, of which waited for: 7 -> 0; matrix products, arithmetic and copies ran while one was open for 5% -> 0% of each run, Pallas kernels for 0% -> 0%
where the time goes in v1:
time: 456 us; the launch traced here: 450 us
  Pallas kernels  221 us (48%)
  other arithmetic  180 us (39%)
  matrix products  23.1 us (5%)
  local copies, waits for them, and re-layouts  20.3 us (4%)
  between operations  6.51 us (1%)
    another operation x30, other arithmetic, per_device(): upper = jnp.linalg.cholesky(gram).T  172 us
    pallas_call x1, Pallas kernels, per_device(): pl.pallas_call(functools.partial(mix_kernel, nx, nz, 1.0 / math.sqrt(loca...  117 us
    pallas_call x1, Pallas kernels, per_device(): pl.pallas_call(functools.partial(gram_kernel, nx, nz, nc, local), out_sha...  104 us
    another operation x14, matrix products, per_device(): upper = jnp.linalg.cholesky(gram).T  23.1 us
    reshape x2, local copies, waits for them, and re-layouts, per_device(): gram.reshape(nc, nx, nc, nz // nc, rows_z, TILE).transpose(2, 1, 3, 4, 0, 5)  9.33 us

profile of v1, /device:TPU:1, one launch (start us, length us, event | category | flops | bytes accessed | tf_op | source)
XLA Modules:
  0.0 450.5 jit_solution(5695408254667160583)
XLA Ops:
  0.6 0.7 convert_bitcast_fusion.sign_ref
  1.3 0.7 fusion.30.key_ref
  2.0 1.2 copy-done
  3.2 117.3 %mix.1 = (f32[64,32,128]{2,1,0:T(8,128)S(1)}, s32[64,1,128]{2,1,0:T(1,128)S(1)}) custom-call(f32[2048,128]{1,0:T(8,128)S(1)} %copy-done, f32[16,128]{1,0:T(8,128)S(1)} %convert_bitcast_fusion.sign_ref, s32[1,128]{1,0:T(1,128)S(1)} %fusion.30.key_ref), custom_call_target="tpu_custom_call" | custom-call | tf_op jit(solution)/shard_map/mix/pallas_call | solution.py:242
  120.5 103.5 %gram.1 = f32[8,4,16,16,128]{4,3,2,1,0:T(8,128)S(1)} custom-call(f32[2048,128]{1,0:T(8,128)S(1)} %bitcast.64, s32[64,128]{1,0:T(8,128)S(1)} %bitcast.66), custom_call_target="tpu_custom_call" | custom-call | tf_op jit(solution)/shard_map/gram/pallas_call | solution.py:258
  224.1 3.8 copy.9
  227.9 3.3 copy.16
  231.2 5.5 %copy.10 = f32[1024,1024]{0,1:T(8,128)} copy(f32[1024,1024]{1,0:T(8,128)} %bitcast.69) | data formatting | bytes 8388608 | tf_op jit(solution)/shard_map/reshape | solution.py:275
  236.7 5.0 %fusion = f32[1024,1024]{1,0:T(8,128)S(1)} fusion(f32[1024,1024]{0,1:T(8,128)} %copy.10, f32[128,8,8,128]{3,2,1,0:T(8,128)} %bitcast.68), kind=kLoop, calls=%fused_computation.2 | loop fusion | flops 2097152 | bytes 12582912 | tf_op jit(solution)/shard_map/jit(cholesky)/div | solution.py:276
  241.8 1.9 copy-done.2
  243.7 11.7 %cholesky.223 = f32[128,128]{1,0:T(8,128)S(1)} custom-call(f32[128,128]{1,0:T(8,128)S(1)} %cholesky.580), custom_call_target="Cholesky" | custom-call | tf_op jit(solution)/shard_map/jit(cholesky)/cholesky | solution.py:276
  255.5 9.8 %custom-call.59 = f32[1,128,128]{1,2,0:T(8,128)S(1)} custom-call(f32[1,128,128]{2,1,0:T(8,128)S(1)} %get-tuple-element.31), custom_call_target="InvertDiagBlocksLowerTriangular" | custom-call | tf_op jit(solution)/shard_map/jit(cholesky)/cholesky | solution.py:276
  265.3 2.5 cholesky.255
  267.8 2.4 constant_dynamic-update-slice_fusion.7
  270.1 1.5 convolution_subtract_fusion
  271.7 12.1 %cholesky.244 = f32[128,128]{1,0:T(8,128)S(1)} custom-call(f32[128,128]{1,0:T(8,128)S(1)} %cholesky.584), custom_call_target="Cholesky" | custom-call | tf_op jit(solution)/shard_map/jit(cholesky)/cholesky | solution.py:276
  283.8 0.6 select_reduce_fusion.6
  286.4 9.8 %custom-call.60 = f32[1,128,128]{1,2,0:T(8,128)S(1)} custom-call(f32[1,128,128]{2,1,0:T(8,128)S(1)} %get-tuple-element.28), custom_call_target="InvertDiagBlocksLowerTriangular" | custom-call | tf_op jit(solution)/shard_map/jit(cholesky)/cholesky | solution.py:276
  296.2 1.2 convolution_dynamic-update-slice_fusion
  297.4 2.1 convolution_subtract_fusion.1
  299.5 11.7 %cholesky.468 = f32[128,128]{1,0:T(8,128)S(1)} custom-call(f32[128,128]{1,0:T(8,128)S(1)} %cholesky.589), custom_call_target="Cholesky" | custom-call | tf_op jit(solution)/shard_map/jit(cholesky)/cholesky | solution.py:276
  313.2 9.8 %custom-call.61 = f32[1,128,128]{1,2,0:T(8,128)S(1)} custom-call(f32[1,128,128]{2,1,0:T(8,128)S(1)} %get-tuple-element.25), custom_call_target="InvertDiagBlocksLowerTriangular" | custom-call | tf_op jit(solution)/shard_map/jit(cholesky)/cholesky | solution.py:276
  323.0 1.2 convolution_dynamic-update-slice_fusion.1
  324.2 2.3 convolution_subtract_fusion.2
  326.5 11.9 %cholesky.487 = f32[128,128]{1,0:T(8,128)S(1)} custom-call(f32[128,128]{1,0:T(8,128)S(1)} %cholesky.594), custom_call_target="Cholesky" | custom-call | tf_op jit(solution)/shard_map/jit(cholesky)/cholesky | solution.py:276
  338.4 0.6 select_reduce_fusion.4
  340.3 9.8 %custom-call.62 = f32[1,128,128]{1,2,0:T(8,128)S(1)} custom-call(f32[1,128,128]{2,1,0:T(8,128)S(1)} %get-tuple-element.22), custom_call_target="InvertDiagBlocksLowerTriangular" | custom-call | tf_op jit(solution)/shard_map/jit(cholesky)/cholesky | solution.py:276
  350.1 1.1 convolution_dynamic-update-slice_fusion.2
  351.2 2.3 convolution_subtract_fusion.3
  353.6 11.7 %cholesky.506 = f32[128,128]{1,0:T(8,128)S(1)} custom-call(f32[128,128]{1,0:T(8,128)S(1)} %cholesky.599), custom_call_target="Cholesky" | custom-call | tf_op jit(solution)/shard_map/jit(cholesky)/cholesky | solution.py:276
  365.3 0.6 select_reduce_fusion.3
  367.2 10.0 %custom-call.63 = f32[1,128,128]{1,2,0:T(8,128)S(1)} custom-call(f32[1,128,128]{2,1,0:T(8,128)S(1)} %get-tuple-element.19), custom_call_target="InvertDiagBlocksLowerTriangular" | custom-call | tf_op jit(solution)/shard_map/jit(cholesky)/cholesky | solution.py:276
  377.2 1.0 convolution_dynamic-update-slice_fusion.3
  378.3 2.3 convolution_subtract_fusion.4
  380.6 11.7 %cholesky.526 = f32[128,128]{1,0:T(8,128)S(1)} custom-call(f32[128,128]{1,0:T(8,128)S(1)} %cholesky.604), custom_call_target="Cholesky" | custom-call | tf_op jit(solution)/shard_map/jit(cholesky)/cholesky | solution.py:276
  394.2 9.8 %custom-call.64 = f32[1,128,128]{1,2,0:T(8,128)S(1)} custom-call(f32[1,128,128]{2,1,0:T(8,128)S(1)} %get-tuple-element.16), custom_call_target="InvertDiagBlocksLowerTriangular" | custom-call | tf_op jit(solution)/shard_map/jit(cholesky)/cholesky | solution.py:276
  404.0 0.9 convolution_dynamic-update-slice_fusion.4
  404.9 2.0 convolution_subtract_fusion.5
  407.0 11.9 %cholesky.546 = f32[128,128]{1,0:T(8,128)S(1)} custom-call(f32[128,128]{1,0:T(8,128)S(1)} %cholesky.609), custom_call_target="Cholesky" | custom-call | tf_op jit(solution)/shard_map/jit(cholesky)/cholesky | solution.py:276
  418.9 0.6 select_reduce_fusion.1
  420.9 9.8 %custom-call.65 = f32[1,128,128]{1,2,0:T(8,128)S(1)} custom-call(f32[1,128,128]{2,1,0:T(8,128)S(1)} %get-tuple-element.13), custom_call_target="InvertDiagBlocksLowerTriangular" | custom-call | tf_op jit(solution)/shard_map/jit(cholesky)/cholesky | solution.py:276
  430.7 0.8 convolution_dynamic-update-slice_fusion.5
  431.5 1.8 convolution_subtract_fusion.6
  433.3 11.7 %cholesky.564 = f32[128,128]{1,0:T(8,128)S(1)} custom-call(f32[128,128]{1,0:T(8,128)S(1)} %convolution_subtract_fusion.6), custom_call_target="Cholesky" | custom-call | tf_op jit(solution)/shard_map/jit(cholesky)/cholesky | solution.py:276
  445.0 0.6 select_reduce_fusion
  447.0 1.1 fusion.7
  448.1 1.0 copy.11
  449.1 1.0 copy.32
  (21 shorter events, 5.8 us)
Async XLA Ops:
  2.0 1.2 copy-start
  227.9 3.3 copy-start.1
  241.8 1.9 copy-start.2

commit v2 on v1

--- a/solution.py
+++ b/solution.py
@@ -225,6 +225,80 @@
     wait_for(gram_ref.at[mc, mx, pl.ds(0, nz - 1)], send_sem.at[3])
     wait_for(gram_ref.at[mc, pl.ds(0, nx - 1)], send_sem.at[4])
     wait_for(gram_ref.at[pl.ds(0, nc - 1)], send_sem.at[5])
+
+
+def left_parts(values):
+    high, middle, low = split_three(values)
+    return jnp.concatenate([high, high, middle, middle, high, low], axis=1)
+
+def right_parts(values):
+    high, middle, low = split_three(values)
+    return jnp.concatenate([high, middle, high, middle, low, high], axis=0)
+
+def over_rows(row):
+    return jnp.broadcast_to(row, (8, TILE))
+
+def inverse(p):
+    r = pl.reciprocal(p, approx=True)
+    return r * (2.0 - p * r)
+
+def factor(block):
+    groups = TILE // 8
+    sub = lax.broadcasted_iota(jnp.int32, (8, TILE), 0)
+    lane = lax.broadcasted_iota(jnp.int32, (8, TILE), 1)
+    s = [block[8 * g:8 * g + 8] for g in range(groups)]
+    e = [jnp.where(sub + 8 * g == lane, 1.0, 0.0) for g in range(groups)]
+    for t in range(groups):
+        cols = [{g: jnp.broadcast_to(s[g][:, 8 * t + j:8 * t + j + 1], (8, TILE)) for g in range(t, groups)} for j in range(8)]
+        pivots = jnp.zeros((8, TILE), F32)
+        for j in range(8):
+            pivot = over_rows(cols[j][t][j:j + 1])
+            pivots = jnp.where(sub == j, pivot, pivots)
+            r = inverse(pivot)
+            heads = {l: over_rows(cols[l][t][j:j + 1]) for l in range(j + 1, 8)}
+            head_s, head_e = over_rows(s[t][j:j + 1]), over_rows(e[t][j:j + 1])
+            for g in range(t, groups):
+                m = cols[j][g] * r
+                if g == t:
+                    m = jnp.where(sub > j, m, 0.0)
+                for l in range(j + 1, 8):
+                    cols[l][g] = cols[l][g] - m * heads[l]
+                s[g] = s[g] - m * head_s
+                e[g] = e[g] - m * head_e
+        root = lax.rsqrt(pivots)
+        s[t] = jnp.where(lane >= sub + 8 * t, s[t] * root, 0.0)
+        e[t] = e[t] * root
+    return jnp.concatenate(s, axis=0), jnp.concatenate(e, axis=0)
+
+def chol_kernel(nc, load, mc, gram_ref, out_ref, work, row, right):
+    def fill(c, carry):
+        for k in range(nc):
+            work[k, :, pl.ds(pl.multiple_of(c * TILE, TILE), TILE)] = load(gram_ref, k, c)
+        return carry
+    lax.fori_loop(0, nc, fill, 0)
+
+    def step(k, carry):
+        own = pl.ds(pl.multiple_of(k * TILE, TILE), TILE)
+        upper, inv = factor(work[k, :, own])
+        left = left_parts(inv)
+        def panel(j, carry):
+            at = pl.ds(pl.multiple_of(j * TILE, TILE), TILE)
+            got = jnp.dot(left, right_parts(work[k, :, at]), preferred_element_type=F32)
+            row[:, at] = got
+            right[:, at] = right_parts(got)
+            return carry
+        lax.fori_loop(k + 1, nc, panel, 0)
+        row[:, own] = upper
+        mine = row[:, pl.ds(pl.multiple_of(mc * TILE, TILE), TILE)]
+        out_ref[pl.ds(pl.multiple_of(k * TILE, TILE), TILE), :] = jnp.where(mc >= k, mine, 0.0)
+        def trail(i, carry):
+            at = pl.ds(pl.multiple_of(i * TILE, TILE), TILE)
+            turned = left_parts(row[:, at].T)
+            work[i] = work[i] - jnp.dot(turned, right[...], preferred_element_type=F32)
+            return carry
+        lax.fori_loop(k + 1, nc, trail, 0)
+        return carry
+    lax.fori_loop(0, nc, step, 0)
 
 
 def params(number):
@@ -272,9 +346,27 @@
         compiler_params=params(1),
         name="gram",
     )(mixed_slab, keys.reshape(n, per_owner))
-    gram = gram.reshape(nc, nx, nc, nz // nc, rows_z, TILE).transpose(2, 1, 3, 4, 0, 5).reshape(nc * TILE, nc * TILE)
-    upper = jnp.linalg.cholesky(gram).T
-    precond = lax.dynamic_slice_in_dim(upper, lax.axis_index("col") * width, width, 1)
+    per_block = nz // nc
+
+    def block(ref, k, c):
+        return ref[c, :, per_block * k:per_block * (k + 1)].reshape(TILE, TILE)
+
+    def root_kernel(gram_ref, out_ref, *scratch):
+        chol_kernel(nc, block, lax.axis_index("col"), gram_ref, out_ref, *scratch)
+
+    precond = pl.pallas_call(
+        root_kernel,
+        out_shape=jax.ShapeDtypeStruct((nc * TILE, width), F32),
+        in_specs=[vmem],
+        out_specs=vmem,
+        scratch_shapes=[
+            pltpu.VMEM((nc, TILE, nc * TILE), F32),
+            pltpu.VMEM((TILE, nc * TILE), F32),
+            pltpu.VMEM((6 * TILE, nc * TILE), BF16),
+        ],
+        compiler_params=pltpu.CompilerParams(vmem_limit_bytes=40 * 2**20),
+        name="root",
+    )(gram)
     return (mixed_slab, precond)
 
 

time: 456 us -> 283 us (0.62); the launches traced: 450 us -> 282 us
  other arithmetic: 180 us -> 1.38 us
  Pallas kernels: 221 us -> 278 us
  matrix products: 23.1 us -> 0 us
  local copies, waits for them, and re-layouts: 20.3 us -> 2.19 us
  between operations: 6.51 us -> 0.65 us
    another operation x30 -> x0, other arithmetic: 172 us -> none  [per_device(): upper = jnp.linalg.cholesky(gram).T]
    pallas_call x0 -> x1, Pallas kernels: none -> 57.3 us  [per_device(): pl.pallas_call(root_kernel, out_shape=jax.ShapeDtypeStruct((nc * TILE, wi...]
    another operation x14 -> x0, matrix products: 23.1 us -> none  [per_device(): upper = jnp.linalg.cholesky(gram).T]
    reshape x2 -> x0, local copies, waits for them, and re-layouts: 9.33 us -> none  [per_device(): gram.reshape(nc, nx, nc, nz // nc, rows_z, TILE).transpose(2, 1, 3, 4, 0, 5)]
    unnamed x9 -> x3, local copies, waits for them, and re-layouts: 8.41 us -> 2.19 us
    div x1 -> x0, other arithmetic: 5.02 us -> none  [per_device(): upper = jnp.linalg.cholesky(gram).T]
where the time goes in v2:
time: 283 us; the launch traced here: 282 us
  Pallas kernels  278 us (98%)
    pallas_call x1, Pallas kernels, per_device(): pl.pallas_call(functools.partial(mix_kernel, nx, nz, 1.0 / math.sqrt(loca...  117 us
    pallas_call x1, Pallas kernels, per_device(): pl.pallas_call(functools.partial(gram_kernel, nx, nz, nc, local), out_sha...  104 us
    pallas_call x1, Pallas kernels, per_device(): pl.pallas_call(root_kernel, out_shape=jax.ShapeDtypeStruct((nc * TILE, wi...  57.3 us

profile of v2, /device:TPU:1, one launch (start us, length us, event | category | flops | bytes accessed | tf_op | source)
XLA Modules:
  0.0 282.3 jit_solution(12143490709824821007)
XLA Ops:
  0.6 0.7 convert_bitcast_fusion.sign_ref
  1.3 0.7 fusion.key_ref
  2.0 0.0 copy-start
  2.0 1.2 copy-done
  3.2 117.3 %mix.1 = (f32[64,32,128]{2,1,0:T(8,128)S(1)}, s32[64,1,128]{2,1,0:T(1,128)S(1)}) custom-call(f32[2048,128]{1,0:T(8,128)S(1)} %copy-done, f32[16,128]{1,0:T(8,128)S(1)} %convert_bitcast_fusion.sign_ref, s32[1,128]{1,0:T(1,128)S(1)} %fusion.key_ref), custom_call_target="tpu_custom_call" | custom-call | tf_op jit(solution)/shard_map/mix/pallas_call | solution.py:316
  120.5 103.5 %gram.1.gram_ref = f32[8,4,16,16,128]{4,3,2,1,0:T(8,128)S(1)} custom-call(f32[2048,128]{1,0:T(8,128)S(1)} %bitcast.10, s32[64,128]{1,0:T(8,128)S(1)} %bitcast.12), custom_call_target="tpu_custom_call" | custom-call | tf_op jit(solution)/shard_map/gram/pallas_call | solution.py:332
  224.1 57.3 %root.1 = f32[1024,128]{1,0:T(8,128)} custom-call(f32[8,4,16,16,128]{4,3,2,1,0:T(8,128)S(1)} %gram.1.gram_ref), custom_call_target="tpu_custom_call" | custom-call | tf_op jit(solution)/shard_map/root/pallas_call | solution.py:357
  281.4 1.0 copy.7
Async XLA Ops:
  2.0 1.2 copy-start

commit v3 on v1

v3 whole, which is shorter than its diff:
```python
import functools
import math

import jax
import jax.numpy as jnp
from jax import lax
from jax.experimental import pallas as pl
from jax.experimental.pallas import tpu as pltpu
from jax.sharding import PartitionSpec as P

MESH = pl.DeviceIdType.MESH
F32, BF16 = jnp.float32, jnp.bfloat16
TILE = 128


def split_three(values):
    high = values.astype(BF16)
    rest = values - high.astype(F32)
    middle = rest.astype(BF16)
    return high, middle, (rest - middle.astype(F32)).astype(BF16)


def exact_dot(left, values):
    return sum(jnp.dot(left, part, preferred_element_type=F32) for part in split_three(values))


def butterfly(items):
    items, apart = list(items), 1
    while apart < len(items):
        for i in range(len(items)):
            if not i & apart:
                items[i], items[i + apart] = items[i] + items[i + apart], items[i] - items[i + apart]
        apart *= 2
    return items


def wait_for(ref, sem):
    pltpu.make_async_copy(ref, ref, sem).wait()


def left_parts(values):
    high, middle, low = split_three(values)
    return jnp.concatenate([high, high, middle, middle, high, low], axis=1)


def right_parts(values):
    high, middle, low = split_three(values)
    return jnp.concatenate([high, middle, high, middle, low, high], axis=0)


def over_rows(row):
    return jnp.broadcast_to(row, (8, TILE))


def inverse(p):
    r = pl.reciprocal(p, approx=True)
    return r * (2.0 - p * r)


def factor(block):
    groups = TILE // 8
    sub = lax.broadcasted_iota(jnp.int32, (8, TILE), 0)
    lane = lax.broadcasted_iota(jnp.int32, (8, TILE), 1)
    s = [block[8 * g:8 * g + 8] for g in range(groups)]
    e = [jnp.where(sub + 8 * g == lane, 1.0, 0.0) for g in range(groups)]
    for t in range(groups):
        cols = [{g: jnp.broadcast_to(s[g][:, 8 * t + j:8 * t + j + 1], (8, TILE)) for g in range(t, groups)} for j in range(8)]
        pivots = jnp.zeros((8, TILE), F32)
        for j in range(8):
            pivot = over_rows(cols[j][t][j:j + 1])
            pivots = jnp.where(sub == j, pivot, pivots)
            r = inverse(pivot)
            heads = {l: over_rows(cols[l][t][j:j + 1]) for l in range(j + 1, 8)}
            head_s, head_e = over_rows(s[t][j:j + 1]), over_rows(e[t][j:j + 1])
            for g in range(t, groups):
                m = cols[j][g] * r
                if g == t:
                    m = jnp.where(sub > j, m, 0.0)
                for l in range(j + 1, 8):
                    cols[l][g] = cols[l][g] - m * heads[l]
                s[g] = s[g] - m * head_s
                e[g] = e[g] - m * head_e
        root = lax.rsqrt(pivots)
        s[t] = jnp.where(lane >= sub + 8 * t, s[t] * root, 0.0)
        e[t] = e[t] * root
    return jnp.concatenate(s, axis=0), jnp.concatenate(e, axis=0)


def chol_kernel(nc, load, mc, gram_ref, out_ref, work, row, right):
    for k in range(nc):
        for c in range(k, nc):
            work[k, :, c * TILE:(c + 1) * TILE] = load(gram_ref, k, c)

    def step(k, carry):
        own = pl.ds(pl.multiple_of(k * TILE, TILE), TILE)
        upper, inv = factor(work[k, :, own])
        left = left_parts(inv)
        def panel(j, carry):
            at = pl.ds(pl.multiple_of(j * TILE, TILE), TILE)
            got = jnp.dot(left, right_parts(work[k, :, at]), preferred_element_type=F32)
            row[:, at] = got
            right[:, at] = right_parts(got)
            return carry
        lax.fori_loop(k + 1, nc, panel, 0)
        row[:, own] = upper
        mine = row[:, pl.ds(pl.multiple_of(mc * TILE, TILE), TILE)]
        out_ref[pl.ds(pl.multiple_of(k * TILE, TILE), TILE), :] = jnp.where(mc >= k, mine, 0.0)
        def trail(i, carry):
            at = pl.ds(pl.multiple_of(i * TILE, TILE), TILE)
            turned = left_parts(row[:, at].T)
            work[i] = work[i] - jnp.dot(turned, right[...], preferred_element_type=F32)
            return carry
        lax.fori_loop(k + 1, nc, trail, 0)
        return carry
    lax.fori_loop(0, nc, step, 0)


class Plan:
    def __init__(self, nx, nz, nc, local, per_owner):
        self.nx, self.nz, self.nc, self.n, self.ny = nx, nz, nc, nx * nz, nc // 2
        self.local, self.samples = local, per_owner * self.n
        self.chunk = local // self.n
        self.pairs = [(k, c) for k in range(nc) for c in range(k, nc)]
        per_x = -(-len(self.pairs) // nx)
        self.per_z = -(-per_x // nz)
        self.owners = -(-per_x // self.per_z)
        self.per_x = self.per_z * self.owners
        self.blocks = nx * self.per_x
        self.strip = TILE // nc


def mix_kernel(
    plan, x_ref, sign_ref, key_ref, out_ref, gram_ref, keys_ref, work, recv, back, gathered, left, right, parts, from_core,
    from_y, over_y, from_x, from_z, send_sem, recv_sem, y_sem,
):
    nx, nz, n, nc, ny, local = plan.nx, plan.nz, plan.n, plan.nc, plan.ny, plan.local
    scale = 1.0 / math.sqrt(local * n)
    blocks, chunk = sign_ref.shape[0], work.shape[1]
    per_block = TILE // chunk
    me, col = lax.axis_index("row"), lax.axis_index("col")
    mx, mz = lax.div(me, nz), lax.rem(me, nz)
    my, core = lax.div(col, 2), lax.rem(col, 2)
    strip = core * ny + my
    sibling = (me, col + 1 - 2 * core)

    def peer(k):
        dx, m = lax.rem(k, nx), lax.div(k, nx)
        dz = nz + lax.div(m + 1, 2) * (2 * lax.rem(m, 2) - 1)
        return lax.rem(mx + dx, nx) * nz + lax.rem(mz + dz, nz)

    barrier = pltpu.get_barrier_semaphore()

    def greet(k, carry):
        pl.semaphore_signal(barrier, inc=1, device_id=(peer(k), col), device_id_type=MESH)
        return carry

    lax.fori_loop(1, n, greet, 0)
    for d in range(1, nc):
        pl.semaphore_signal(barrier, inc=1, device_id=(me, lax.rem(col + d, nc)), device_id_type=MESH)

    shared = lax.broadcasted_iota(jnp.int32, (TILE, TILE), 0) & lax.broadcasted_iota(jnp.int32, (TILE, TILE), 1)
    shared = shared ^ shared >> 4
    shared = shared ^ shared >> 2
    shared = shared ^ shared >> 1
    table = (1 - 2 * (shared & 1)).astype(F32)

    def inner(a, carry):
        left = (table * sign_ref[pl.ds(a, 1), :]).astype(BF16)
        rows = x_ref[pl.ds(pl.multiple_of(a * TILE, TILE), TILE), :]
        work[pl.ds(a * per_block, per_block)] = exact_dot(left, rows).reshape(per_block, chunk, TILE)
        return carry

    lax.fori_loop(0, blocks, inner, 0)

    def outer(b, carry):
        part, at = lax.div(b * 8, chunk), pl.multiple_of(lax.rem(b * 8, chunk), 8)
        mixed = butterfly([work[a * per_block + part, pl.ds(at, 8), :] for a in range(blocks)])
        for a in range(blocks):
            work[a * per_block + part, pl.ds(at, 8), :] = mixed[a]
        return carry

    lax.fori_loop(0, TILE // 8, outer, 0)
    pl.semaphore_wait(barrier, n + nc - 2)

    def send(src, dst, device, which, arrival=None):
        pltpu.make_async_remote_copy(
            src_ref=src, dst_ref=dst, send_sem=send_sem.at[which],
            recv_sem=recv_sem.at[which] if arrival is None else arrival,
            device_id=device, device_id_type=MESH,
        ).start()

    def there(k, carry):
        device = (peer(k), col)
        send(key_ref, keys_ref.at[me], device, 0)
        send(work.at[device[0]], recv.at[me], device, 1)
        return carry

    lax.fori_loop(1, n, there, 0)
    keys_ref[me] = key_ref[...]
    recv[me] = work[me]

    per_col = n // nc
    rows = per_col * plan.chunk
    wait_for(keys_ref.at[pl.ds(0, n - 1)], recv_sem.at[0])
    bins = lax.broadcasted_iota(jnp.int32, (rows, TILE), 0)

    def count(o, total):
        key = keys_ref[o]
        holder, offset = key // local - col * per_col, key % local - me * plan.chunk
        here = (holder >= 0) & (holder < per_col) & (offset >= 0) & (offset < plan.chunk)
        where = jnp.where(here, holder * plan.chunk + offset, -1)
        return total + jnp.where(bins == where, 1.0, 0.0)

    counts = jnp.sum(lax.fori_loop(0, n, count, jnp.zeros((rows, TILE), F32)), axis=1, keepdims=True)
    wait_for(recv.at[pl.ds(0, n - 1)], recv_sem.at[1])
    radix = min(8, n)

    def low(g, carry):
        mixed = butterfly([recv[radix * g + i] for i in range(radix)])
        for i in range(radix):
            recv[radix * g + i] = mixed[i]
        return carry

    def high(i, carry):
        mixed = butterfly([recv[radix * g + i] for g in range(n // radix)])
        for g in range(n // radix):
            back[radix * g + i] = mixed[g] * scale
        return carry

    lax.fori_loop(0, n // radix, low, 0)
    lax.fori_loop(0, radix, high, 0)

    for d in range(1, nc):
        to = lax.rem(col + d, nc)
        send(back.at[pl.ds(to * per_col, per_col)], gathered.at[col], (me, to), 3)

    def home(k, carry):
        device = peer(k)
        send(back.at[device], out_ref.at[me], (device, col), 2)
        return carry

    lax.fori_loop(1, n, home, 0)
    out_ref[me] = back[me]
    gathered[col] = back[pl.ds(col * per_col, per_col)]
    wait_for(gathered.at[pl.ds(0, nc - 1)], recv_sem.at[3])

    for c in range(nc):
        here = gathered[c].reshape(rows, TILE)
        right[:, c * TILE:(c + 1) * TILE] = right_parts(here)
        left[c * TILE:(c + 1) * TILE, :] = left_parts((here * counts).T)
    for first in range(0, nc, 2):
        wide = jnp.dot(left[:(first + 2) * TILE, :], right[:, first * TILE:(first + 2) * TILE], preferred_element_type=F32)
        for c in (first, first + 1):
            for k in range(c + 1):
                block = wide[k * TILE:(k + 1) * TILE, (c - first) * TILE:(c - first + 1) * TILE]
                parts[:, plan.pairs.index((k, c))] = block.reshape(nc, plan.strip, TILE)

    send(parts.at[pl.ds((1 - core) * ny, ny)], from_core, sibling, 4)
    wait_for(from_core, recv_sem.at[4])

    def pair(q, carry):
        over_y[q] = parts[core * ny + q] + from_core[q]
        return carry

    lax.fori_loop(0, ny, pair, 0)
    for d in range(1, ny):
        to = lax.rem(my + d, ny)
        send(over_y.at[to], from_y.at[my], (me, to * 2 + core), 5)
    from_y[my] = over_y[my]
    if ny > 1:
        wait_for(from_y.at[pl.ds(0, ny - 1)], recv_sem.at[5])
    own = over_y.at[my]
    total = from_y[0]
    for q in range(1, ny):
        total = total + from_y[q]
    if ny > 1:
        wait_for(over_y.at[pl.ds(0, ny - 1)], send_sem.at[5])
    over_y[my] = total

    def share(q):
        return own.at[pl.ds(q * plan.per_x, plan.per_x)]

    for d in range(1, nx):
        to = lax.rem(mx + d, nx)
        send(share(to), from_x.at[mx], (to * nz + mz, col), 6)
    from_x[mx] = over_y[my, pl.ds(mx * plan.per_x, plan.per_x)]
    wait_for(from_x.at[pl.ds(0, nx - 1)], recv_sem.at[6])
    total = from_x[0]
    for q in range(1, nx):
        total = total + from_x[q]
    wait_for(from_x.at[pl.ds(0, nx - 1)], send_sem.at[6])
    from_x[mx] = total
    slot = plan.per_z

    def piece(ref, q):
        return ref.at[pl.ds(q * slot, slot)]

    for q in range(plan.owners):
        @pl.when(mz != q)
        def _():
            send(piece(from_x.at[mx], q), from_z.at[mz], (mx * nz + q, col), 7)

    @pl.when(mz < plan.owners)
    def _():
        from_z[mz] = from_x[mx, pl.ds(mz * slot, slot)]
        wait_for(from_z.at[pl.ds(0, nz - 1)], recv_sem.at[7])
        total = from_z[0]
        for q in range(1, nz):
            total = total + from_z[q]
        gram_ref[strip, pl.ds(mx * plan.per_x + mz * slot, slot)] = total * (1.0 / plan.samples)
        mine = gram_ref.at[strip, pl.ds(mx * plan.per_x + mz * slot, slot)]
        for d in range(1, nz):
            send(mine, mine, (mx * nz + lax.rem(mz + d, nz), col), 8)
        if plan.owners > 1:
            wait_for(gram_ref.at[strip, pl.ds(0, plan.per_x - slot)], recv_sem.at[8])

    @pl.when(mz >= plan.owners)
    def _():
        other = gram_ref.at[strip, pl.ds(mx * plan.per_x, plan.per_x)]
        wait_for(other, recv_sem.at[8])

    mine = gram_ref.at[strip, pl.ds(mx * plan.per_x, plan.per_x)]
    for d in range(1, nx):
        send(mine, mine, (lax.rem(mx + d, nx) * nz + mz, col), 9)
    wait_for(gram_ref.at[strip, pl.ds(0, plan.blocks - plan.per_x)], recv_sem.at[9])
    mine = gram_ref.at[strip]
    send(mine, mine, sibling, 11)
    for d in range(1, ny):
        send(mine, mine, (me, lax.rem(my + d, ny) * 2 + core), 10, y_sem.at[my])
    for d in range(1, ny):
        q = lax.rem(my + d, ny)
        other = gram_ref.at[core * ny + q]
        wait_for(other, y_sem.at[q])
        send(other, other, sibling, 11)
    wait_for(gram_ref.at[pl.ds(0, ny)], recv_sem.at[11])

    wait_for(out_ref.at[pl.ds(0, n - 1)], recv_sem.at[2])
    wait_for(keys_ref.at[pl.ds(0, n - 1)], send_sem.at[0])
    wait_for(recv.at[pl.ds(0, n - 1)], send_sem.at[1])
    wait_for(out_ref.at[pl.ds(0, n - 1)], send_sem.at[2])
    wait_for(gathered.at[pl.ds(0, nc - 1)], send_sem.at[3])
    wait_for(from_core, send_sem.at[4])
    @pl.when(mz < plan.owners)
    def _():
        if plan.owners > 1:
            wait_for(from_x.at[0, pl.ds(0, (plan.owners - 1) * slot)], send_sem.at[7])
        wait_for(from_z.at[pl.ds(0, nz - 1)], send_sem.at[8])

    @pl.when(mz >= plan.owners)
    def _():
        wait_for(from_x.at[0], send_sem.at[7])

    wait_for(gram_ref.at[strip, pl.ds(0, plan.blocks - plan.per_x)], send_sem.at[9])
    if ny > 1:
        wait_for(gram_ref.at[pl.ds(0, ny - 1)], send_sem.at[10])
    wait_for(gram_ref.at[pl.ds(0, ny)], send_sem.at[11])


def per_device(nx, nz, nc, slab_rows, row_flips, sample_holder, sample_offset):
    local, width = slab_rows.shape
    per_owner = sample_offset.shape[0]
    plan = Plan(nx, nz, nc, local, per_owner)
    n, ny, chunk, strip = plan.n, plan.ny, plan.chunk, plan.strip
    rows = n // nc * chunk
    vmem = pl.BlockSpec(memory_space=pltpu.VMEM)
    signs = (1 - 2 * row_flips).astype(F32).reshape(local // TILE, TILE)
    key = (sample_holder[:, 0] * local + sample_offset).reshape(1, per_owner)

    def buffer(*shape, dtype=F32):
        return pltpu.VMEM(shape, dtype)

    mixed, gram = pl.pallas_call(
        functools.partial(mix_kernel, plan),
        out_shape=(
            jax.ShapeDtypeStruct((n, chunk, width), F32),
            jax.ShapeDtypeStruct((nc, plan.blocks, strip, TILE), F32),
        ),
        in_specs=[vmem] * 3,
        out_specs=(vmem, vmem),
        scratch_shapes=[
            buffer(n, 1, per_owner, dtype=jnp.int32),
            buffer(n, chunk, width),
            buffer(n, chunk, width),
            buffer(n, chunk, width),
            buffer(nc, n // nc, chunk, width),
            buffer(nc * TILE, 6 * rows, dtype=BF16),
            buffer(6 * rows, nc * TILE, dtype=BF16),
            buffer(nc, plan.blocks, strip, TILE),
            buffer(ny, plan.blocks, strip, TILE),
            buffer(ny, plan.blocks, strip, TILE),
            buffer(ny, plan.blocks, strip, TILE),
            buffer(nx, plan.per_x, strip, TILE),
            buffer(nz, plan.per_z, strip, TILE),
            pltpu.SemaphoreType.DMA((12,)),
            pltpu.SemaphoreType.DMA((12,)),
            pltpu.SemaphoreType.DMA((ny,)),
        ],
        compiler_params=pltpu.CompilerParams(collective_id=0, has_side_effects=True, vmem_limit_bytes=48 * 2**20),
        name="mix",
    )(slab_rows, signs, key)

    def block(ref, k, c):
        return ref[:, plan.pairs.index((k, c))].reshape(TILE, TILE)

    def root_kernel(gram_ref, out_ref, *scratch):
        chol_kernel(nc, block, lax.axis_index("col"), gram_ref, out_ref, *scratch)

    precond = pl.pallas_call(
        root_kernel,
        out_shape=jax.ShapeDtypeStruct((nc * TILE, width), F32),
        in_specs=[vmem],
        out_specs=vmem,
        scratch_shapes=[
            buffer(nc, TILE, nc * TILE),
            buffer(TILE, nc * TILE),
            buffer(6 * TILE, nc * TILE, dtype=BF16),
        ],
        compiler_params=pltpu.CompilerParams(vmem_limit_bytes=40 * 2**20),
        name="root",
    )(gram)
    return (mixed.reshape(local, width), precond)


def solution(mesh):
    nx = 4
    nz = mesh.shape["row"] // nx
    in_specs = (P("row", "col"), P("row"), P("row", None), P("row"))
    out_specs = (P("row", "col"), P(None, "col"))
    return jax.shard_map(
        functools.partial(per_device, nx, nz, mesh.shape["col"]),
        mesh=mesh, in_specs=in_specs, out_specs=out_specs, check_vma=False,
    )
```

time: 456 us -> 215 us (0.47)
  other arithmetic: 180 us -> 1.38 us
  matrix products: 23.1 us -> 0 us
  local copies, waits for them, and re-layouts: 20.3 us -> 2.19 us
  Pallas kernels: 221 us -> 209 us
  between operations: 6.51 us -> 0.64 us
    another operation x30 -> x0, other arithmetic: 172 us -> none  [per_device(): upper = jnp.linalg.cholesky(gram).T]
    another operation x14 -> x0, matrix products: 23.1 us -> none  [per_device(): upper = jnp.linalg.cholesky(gram).T]
    pallas_call x2, Pallas kernels: 221 us -> 209 us  [the longest x1 152 us: per_device(): pl.pallas_call(functools.partial(mix_kernel, plan), out_shape=(jax.ShapeD...]
    reshape x2 -> x0, local copies, waits for them, and re-layouts: 9.33 us -> none  [per_device(): gram.reshape(nc, nx, nc, nz // nc, rows_z, TILE).transpose(2, 1, 3, 4, 0, 5)]
    unnamed x9 -> x3, local copies, waits for them, and re-layouts: 8.41 us -> 2.19 us
    div x1 -> x0, other arithmetic: 5.02 us -> none  [per_device(): upper = jnp.linalg.cholesky(gram).T]
where the time goes in v3:
time: 215 us; the launch traced here: 213 us
  Pallas kernels  209 us (97%)
  local copies, waits for them, and re-layouts  2.19 us (1%)
    pallas_call x1, Pallas kernels, per_device(): pl.pallas_call(functools.partial(mix_kernel, plan), out_shape=(jax.ShapeD...  152 us
    pallas_call x1, Pallas kernels, per_device(): pl.pallas_call(root_kernel, out_shape=jax.ShapeDtypeStruct((nc * TILE, wi...  57 us

profile of v3, /device:TPU:1, one launch (start us, length us, event | category | flops | bytes accessed | tf_op | source)
XLA Modules:
  0.0 213.4 jit_solution(8616576279365003125)
XLA Ops:
  0.6 0.7 fusion.key_ref
  1.3 0.7 convert_bitcast_fusion.sign_ref
  2.0 0.0 copy-start
  2.0 1.2 copy-done
  3.2 152.2 %mix.1 = (f32[64,32,128]{2,1,0:T(8,128)S(1)}, f32[8,36,16,128]{3,2,1,0:T(8,128)S(1)}) custom-call(f32[2048,128]{1,0:T(8,128)S(1)} %copy-done, f32[16,128]{1,0:T(8,128)S(1)} %convert_bitcast_fusion.sign_ref, s32[1,128]{1,0:T(1,128)S(1)} %fusion.key_ref), custom_call_target="tpu_custom_call" | custom-call | tf_op jit(solution)/shard_map/mix/pallas_call | solution.py:372
  155.4 57.0 %root.1 = f32[1024,128]{1,0:T(8,128)} custom-call(f32[8,36,16,128]{3,2,1,0:T(8,128)S(1)} %get-tuple-element.5.gram_ref), custom_call_target="tpu_custom_call" | custom-call | tf_op jit(solution)/shard_map/root/pallas_call | solution.py:408
  212.4 1.0 copy.7
Async XLA Ops:
  2.0 1.2 copy-start

commit v4 on v3

--- a/solution.py
+++ b/solution.py
@@ -48,70 +48,63 @@
     return jnp.concatenate([high, middle, high, middle, low, high], axis=0)
 
 
-def over_rows(row):
-    return jnp.broadcast_to(row, (8, TILE))
-
-
-def inverse(p):
-    r = pl.reciprocal(p, approx=True)
-    return r * (2.0 - p * r)
-
-
 def factor(block):
-    groups = TILE // 8
     sub = lax.broadcasted_iota(jnp.int32, (8, TILE), 0)
     lane = lax.broadcasted_iota(jnp.int32, (8, TILE), 1)
-    s = [block[8 * g:8 * g + 8] for g in range(groups)]
-    e = [jnp.where(sub + 8 * g == lane, 1.0, 0.0) for g in range(groups)]
-    for t in range(groups):
-        cols = [{g: jnp.broadcast_to(s[g][:, 8 * t + j:8 * t + j + 1], (8, TILE)) for g in range(t, groups)} for j in range(8)]
+    row = lax.broadcasted_iota(jnp.int32, (TILE, TILE), 0)
+    s, e = block, jnp.where(row == lax.broadcasted_iota(jnp.int32, (TILE, TILE), 1), 1.0, 0.0)
+    upper, inverse = [], []
+    for t in range(TILE // 8):
+        rows = s.shape[0]
+        cols = [jnp.broadcast_to(s[:, 8 * t + j:8 * t + j + 1], (rows, TILE)) for j in range(8)]
         pivots = jnp.zeros((8, TILE), F32)
         for j in range(8):
-            pivot = over_rows(cols[j][t][j:j + 1])
+            pivot = jnp.broadcast_to(cols[j][j:j + 1], (8, TILE))
             pivots = jnp.where(sub == j, pivot, pivots)
-            r = inverse(pivot)
-            heads = {l: over_rows(cols[l][t][j:j + 1]) for l in range(j + 1, 8)}
-            head_s, head_e = over_rows(s[t][j:j + 1]), over_rows(e[t][j:j + 1])
-            for g in range(t, groups):
-                m = cols[j][g] * r
-                if g == t:
-                    m = jnp.where(sub > j, m, 0.0)
-                for l in range(j + 1, 8):
-                    cols[l][g] = cols[l][g] - m * heads[l]
-                s[g] = s[g] - m * head_s
-                e[g] = e[g] - m * head_e
+            r = pl.reciprocal(pivot, approx=True)
+            r = r * (2.0 - pivot * r)
+            m = jnp.where(row[:rows] > j, cols[j] * r[0:1], 0.0)
+            for l in range(j + 1, 8):
+                cols[l] = cols[l] - m * cols[l][j:j + 1]
+            s, e = s - m * s[j:j + 1], e - m * e[j:j + 1]
         root = lax.rsqrt(pivots)
-        s[t] = jnp.where(lane >= sub + 8 * t, s[t] * root, 0.0)
-        e[t] = e[t] * root
-    return jnp.concatenate(s, axis=0), jnp.concatenate(e, axis=0)
-
-
-def chol_kernel(nc, load, mc, gram_ref, out_ref, work, row, right):
+        upper.append(jnp.where(lane >= sub + 8 * t, s[:8] * root, 0.0))
+        inverse.append(e[:8] * root)
+        s, e = s[8:], e[8:]
+    return jnp.concatenate(upper, axis=0), jnp.concatenate(inverse, axis=0)
+
+
+def root_of(nc, load, mc, out_ref, table, left, right):
     for k in range(nc):
         for c in range(k, nc):
-            work[k, :, c * TILE:(c + 1) * TILE] = load(gram_ref, k, c)
-
-    def step(k, carry):
-        own = pl.ds(pl.multiple_of(k * TILE, TILE), TILE)
-        upper, inv = factor(work[k, :, own])
-        left = left_parts(inv)
-        def panel(j, carry):
-            at = pl.ds(pl.multiple_of(j * TILE, TILE), TILE)
-            got = jnp.dot(left, right_parts(work[k, :, at]), preferred_element_type=F32)
-            row[:, at] = got
-            right[:, at] = right_parts(got)
-            return carry
-        lax.fori_loop(k + 1, nc, panel, 0)
-        row[:, own] = upper
-        mine = row[:, pl.ds(pl.multiple_of(mc * TILE, TILE), TILE)]
-        out_ref[pl.ds(pl.multiple_of(k * TILE, TILE), TILE), :] = jnp.where(mc >= k, mine, 0.0)
-        def trail(i, carry):
-            at = pl.ds(pl.multiple_of(i * TILE, TILE), TILE)
-            turned = left_parts(row[:, at].T)
-            work[i] = work[i] - jnp.dot(turned, right[...], preferred_element_type=F32)
-            return carry
-        lax.fori_loop(k + 1, nc, trail, 0)
-        return carry
+            table[k * TILE:(k + 1) * TILE, c * TILE:(c + 1) * TILE] = load(k, c)
+
+    def step(i, carry):
+        at = pl.ds(pl.multiple_of(i * TILE, TILE), TILE)
+        upper, inverse = factor(table[at, at])
+        out_ref[at, :] = jnp.where(mc == i, upper, 0.0)
+        first = left_parts(inverse)
+        for k in range(nc - 1):
+            @pl.when(i == k)
+            def _():
+                end = (k + 1) * TILE
+                row = jnp.dot(first, right_parts(table[k * TILE:end, end:]), preferred_element_type=F32)
+                right[:6 * TILE, end:] = right_parts(row)
+                for c in range(k + 1, nc):
+                    block = row[:, (c - k - 1) * TILE:(c - k) * TILE]
+                    left[c * TILE:(c + 1) * TILE, :6 * TILE] = left_parts(block.T)
+
+                    @pl.when(mc == c)
+                    def _():
+                        out_ref[k * TILE:end, :] = block
+                for c in range((k + 1) // 2 * 2, nc, 2):
+                    cols = slice(max(c, k + 1) * TILE, (c + 2) * TILE)
+                    rows = slice(end, (c + 2) * TILE)
+                    table[rows, cols] = table[rows, cols] - jnp.dot(
+                        left[rows, :6 * TILE], right[:6 * TILE, cols], preferred_element_type=F32
+                    )
+        return carry
+
     lax.fori_loop(0, nc, step, 0)
 
 
@@ -130,7 +123,7 @@
 
 
 def mix_kernel(
-    plan, x_ref, sign_ref, key_ref, out_ref, gram_ref, keys_ref, work, recv, back, gathered, left, right, parts, from_core,
+    plan, x_ref, sign_ref, key_ref, out_ref, root_ref, keys_ref, gram_ref, table, work, recv, back, gathered, left, right, parts, from_core,
     from_y, over_y, from_x, from_z, send_sem, recv_sem, y_sem,
 ):
     nx, nz, n, nc, ny, local = plan.nx, plan.nz, plan.n, plan.nc, plan.ny, plan.local
@@ -162,12 +155,12 @@
     shared = shared ^ shared >> 4
     shared = shared ^ shared >> 2
     shared = shared ^ shared >> 1
-    table = (1 - 2 * (shared & 1)).astype(F32)
+    hadamard = (1 - 2 * (shared & 1)).astype(F32)
 
     def inner(a, carry):
-        left = (table * sign_ref[pl.ds(a, 1), :]).astype(BF16)
+        signed = (hadamard * sign_ref[pl.ds(a, 1), :]).astype(BF16)
         rows = x_ref[pl.ds(pl.multiple_of(a * TILE, TILE), TILE), :]
-        work[pl.ds(a * per_block, per_block)] = exact_dot(left, rows).reshape(per_block, chunk, TILE)
+        work[pl.ds(a * per_block, per_block)] = exact_dot(signed, rows).reshape(per_block, chunk, TILE)
         return carry
 
     lax.fori_loop(0, blocks, inner, 0)
@@ -234,12 +227,6 @@
         to = lax.rem(col + d, nc)
         send(back.at[pl.ds(to * per_col, per_col)], gathered.at[col], (me, to), 3)
 
-    def home(k, carry):
-        device = peer(k)
-        send(back.at[device], out_ref.at[me], (device, col), 2)
-        return carry
-
-    lax.fori_loop(1, n, home, 0)
     out_ref[me] = back[me]
     gathered[col] = back[pl.ds(col * per_col, per_col)]
     wait_for(gathered.at[pl.ds(0, nc - 1)], recv_sem.at[3])
@@ -332,7 +319,18 @@
         other = gram_ref.at[core * ny + q]
         wait_for(other, y_sem.at[q])
         send(other, other, sibling, 11)
+    def home(k, carry):
+        device = peer(k)
+        send(back.at[device], out_ref.at[me], (device, col), 2)
+        return carry
+
+    lax.fori_loop(1, n, home, 0)
     wait_for(gram_ref.at[pl.ds(0, ny)], recv_sem.at[11])
+
+    def block(k, c):
+        return gram_ref[:, plan.pairs.index((k, c))].reshape(TILE, TILE)
+
+    root_of(nc, block, col, root_ref, table, left, right)
 
     wait_for(out_ref.at[pl.ds(0, n - 1)], recv_sem.at[2])
     wait_for(keys_ref.at[pl.ds(0, n - 1)], send_sem.at[0])
@@ -369,16 +367,18 @@
     def buffer(*shape, dtype=F32):
         return pltpu.VMEM(shape, dtype)
 
-    mixed, gram = pl.pallas_call(
+    mixed, precond = pl.pallas_call(
         functools.partial(mix_kernel, plan),
         out_shape=(
             jax.ShapeDtypeStruct((n, chunk, width), F32),
-            jax.ShapeDtypeStruct((nc, plan.blocks, strip, TILE), F32),
+            jax.ShapeDtypeStruct((nc * TILE, width), F32),
         ),
         in_specs=[vmem] * 3,
         out_specs=(vmem, vmem),
         scratch_shapes=[
             buffer(n, 1, per_owner, dtype=jnp.int32),
+            buffer(nc, plan.blocks, strip, TILE),
+            buffer(nc * TILE, nc * TILE),
             buffer(n, chunk, width),
             buffer(n, chunk, width),
             buffer(n, chunk, width),
@@ -399,25 +399,6 @@
         name="mix",
     )(slab_rows, signs, key)
 
-    def block(ref, k, c):
-        return ref[:, plan.pairs.index((k, c))].reshape(TILE, TILE)
-
-    def root_kernel(gram_ref, out_ref, *scratch):
-        chol_kernel(nc, block, lax.axis_index("col"), gram_ref, out_ref, *scratch)
-
-    precond = pl.pallas_call(
-        root_kernel,
-        out_shape=jax.ShapeDtypeStruct((nc * TILE, width), F32),
-        in_specs=[vmem],
-        out_specs=vmem,
-        scratch_shapes=[
-            buffer(nc, TILE, nc * TILE),
-            buffer(TILE, nc * TILE),
-            buffer(6 * TILE, nc * TILE, dtype=BF16),
-        ],
-        compiler_params=pltpu.CompilerParams(vmem_limit_bytes=40 * 2**20),
-        name="root",
-    )(gram)
     return (mixed.reshape(local, width), precond)
 
 

time: 215 us -> 200 us (0.930)
  Pallas kernels: 209 us -> 195 us
    pallas_call x1 -> x0, Pallas kernels: 57 us -> none  [per_device(): pl.pallas_call(root_kernel, out_shape=jax.ShapeDtypeStruct((nc * TILE, wi...]
    pallas_call x1, Pallas kernels: 152 us -> 195 us  [per_device(): pl.pallas_call(functools.partial(mix_kernel, plan), out_shape=(jax.ShapeD...]
where the time goes in v4:
time: 200 us
  Pallas kernels  195 us (98%)
  local copies, waits for them, and re-layouts  2.99 us (1%)
    pallas_call x1, Pallas kernels, per_device(): pl.pallas_call(functools.partial(mix_kernel, plan), out_shape=(jax.ShapeD...  195 us

profile of v4, /device:TPU:1, one launch (start us, length us, event | category | flops | bytes accessed | tf_op | source)
XLA Modules:
  0.0 200.3 jit_solution(13785260361417640873)
XLA Ops:
  0.6 0.7 fusion.key_ref
  1.3 0.7 convert_bitcast_fusion.sign_ref
  2.0 0.0 copy-start
  2.0 1.2 copy-done
  3.2 195.3 %mix.1 = (f32[64,32,128]{2,1,0:T(8,128)S(1)}, f32[1024,128]{1,0:T(8,128)S(1)}) custom-call(f32[2048,128]{1,0:T(8,128)S(1)} %copy-done, f32[16,128]{1,0:T(8,128)S(1)} %convert_bitcast_fusion.sign_ref, s32[1,128]{1,0:T(1,128)S(1)} %fusion.key_ref), custom_call_target="tpu_custom_call" | custom-call | tf_op jit(solution)/shard_map/mix/pallas_call | solution.py:370
  198.5 1.0 copy.8
  199.5 0.8 copy.9
Async XLA Ops:
  2.0 1.2 copy-start

commit v5 on v4

--- a/solution.py
+++ b/solution.py
@@ -61,9 +61,8 @@
         for j in range(8):
             pivot = jnp.broadcast_to(cols[j][j:j + 1], (8, TILE))
             pivots = jnp.where(sub == j, pivot, pivots)
-            r = pl.reciprocal(pivot, approx=True)
-            r = r * (2.0 - pivot * r)
-            m = jnp.where(row[:rows] > j, cols[j] * r[0:1], 0.0)
+            r = pltpu.reciprocal(pivot, approx=True)
+            m = jnp.where(row[:rows] > j, cols[j], 0.0) * r[0:1]
             for l in range(j + 1, 8):
                 cols[l] = cols[l] - m * cols[l][j:j + 1]
             s, e = s - m * s[j:j + 1], e - m * e[j:j + 1]
@@ -118,17 +117,19 @@
         self.per_z = -(-per_x // nz)
         self.owners = -(-per_x // self.per_z)
         self.per_x = self.per_z * self.owners
+        cuts = [self.owners * i // 3 for i in range(4)]
+        self.spans = [(low, high) for low, high in zip(cuts, cuts[1:]) if high > low]
         self.blocks = nx * self.per_x
         self.strip = TILE // nc
 
 
 def mix_kernel(
-    plan, x_ref, sign_ref, key_ref, out_ref, root_ref, keys_ref, gram_ref, table, work, recv, back, gathered, left, right, parts, from_core,
-    from_y, over_y, from_x, from_z, send_sem, recv_sem, y_sem,
+    plan, x_ref, flip_ref, holder_ref, offset_ref, out_ref, root_ref, keys_ref, gram_ref, table, work, recv, back, gathered, left, right, parts, from_core,
+    over_y, from_plane, summed, from_z, send_sem, recv_sem,
 ):
     nx, nz, n, nc, ny, local = plan.nx, plan.nz, plan.n, plan.nc, plan.ny, plan.local
     scale = 1.0 / math.sqrt(local * n)
-    blocks, chunk = sign_ref.shape[0], work.shape[1]
+    blocks, chunk = flip_ref.shape[0], work.shape[1]
     per_block = TILE // chunk
     me, col = lax.axis_index("row"), lax.axis_index("col")
     mx, mz = lax.div(me, nz), lax.rem(me, nz)
@@ -158,7 +159,7 @@
     hadamard = (1 - 2 * (shared & 1)).astype(F32)
 
     def inner(a, carry):
-        signed = (hadamard * sign_ref[pl.ds(a, 1), :]).astype(BF16)
+        signed = (hadamard * (1 - 2 * flip_ref[pl.ds(a, 1), :]).astype(F32)).astype(BF16)
         rows = x_ref[pl.ds(pl.multiple_of(a * TILE, TILE), TILE), :]
         work[pl.ds(a * per_block, per_block)] = exact_dot(signed, rows).reshape(per_block, chunk, TILE)
         return carry
@@ -175,21 +176,20 @@
     lax.fori_loop(0, TILE // 8, outer, 0)
     pl.semaphore_wait(barrier, n + nc - 2)
 
-    def send(src, dst, device, which, arrival=None):
+    def send(src, dst, device, which):
         pltpu.make_async_remote_copy(
-            src_ref=src, dst_ref=dst, send_sem=send_sem.at[which],
-            recv_sem=recv_sem.at[which] if arrival is None else arrival,
+            src_ref=src, dst_ref=dst, send_sem=send_sem.at[which], recv_sem=recv_sem.at[which],
             device_id=device, device_id_type=MESH,
         ).start()
 
     def there(k, carry):
         device = (peer(k), col)
-        send(key_ref, keys_ref.at[me], device, 0)
+        send(keys_ref.at[me], keys_ref.at[me], device, 0)
         send(work.at[device[0]], recv.at[me], device, 1)
         return carry
 
+    keys_ref[me] = holder_ref[...] * local + offset_ref[...]
     lax.fori_loop(1, n, there, 0)
-    keys_ref[me] = key_ref[...]
     recv[me] = work[me]
 
     per_col = n // nc
@@ -250,82 +250,80 @@
         return carry
 
     lax.fori_loop(0, ny, pair, 0)
-    for d in range(1, ny):
-        to = lax.rem(my + d, ny)
-        send(over_y.at[to], from_y.at[my], (me, to * 2 + core), 5)
-    from_y[my] = over_y[my]
-    if ny > 1:
-        wait_for(from_y.at[pl.ds(0, ny - 1)], recv_sem.at[5])
-    own = over_y.at[my]
-    total = from_y[0]
-    for q in range(1, ny):
-        total = total + from_y[q]
-    if ny > 1:
-        wait_for(over_y.at[pl.ds(0, ny - 1)], send_sem.at[5])
-    over_y[my] = total
-
-    def share(q):
-        return own.at[pl.ds(q * plan.per_x, plan.per_x)]
-
-    for d in range(1, nx):
-        to = lax.rem(mx + d, nx)
-        send(share(to), from_x.at[mx], (to * nz + mz, col), 6)
-    from_x[mx] = over_y[my, pl.ds(mx * plan.per_x, plan.per_x)]
-    wait_for(from_x.at[pl.ds(0, nx - 1)], recv_sem.at[6])
-    total = from_x[0]
-    for q in range(1, nx):
-        total = total + from_x[q]
-    wait_for(from_x.at[pl.ds(0, nx - 1)], send_sem.at[6])
-    from_x[mx] = total
+    plane = nx * ny
+
+    def across(d):
+        to_x, to_y = lax.rem(mx + d // ny, nx), lax.rem(my + d % ny, ny)
+        return to_x, to_y, (to_x * nz + mz, to_y * 2 + core)
+
     slot = plan.per_z
 
-    def piece(ref, q):
-        return ref.at[pl.ds(q * slot, slot)]
-
-    for q in range(plan.owners):
-        @pl.when(mz != q)
+    def span(p, x=None):
+        low, high = plan.spans[p]
+        return pl.ds((0 if x is None else x * plan.per_x) + low * slot, (high - low) * slot)
+
+    def owner(p):
+        return (mz >= plan.spans[p][0]) & (mz < plan.spans[p][1])
+
+    stages = range(len(plan.spans))
+    for p in stages:
+        for d in range(1, plane):
+            to_x, to_y, device = across(d)
+            send(over_y.at[to_y, span(p, to_x)], from_plane.at[mx * ny + my, span(p)], device, 9 + p)
+    from_plane[mx * ny + my] = over_y[my, pl.ds(mx * plan.per_x, plan.per_x)]
+    for p in stages:
+        wait_for(from_plane.at[pl.ds(0, plane - 1), span(p)], recv_sem.at[9 + p])
+        total = from_plane[0, span(p)]
+        for q in range(1, plane):
+            total = total + from_plane[q, span(p)]
+        summed[span(p)] = total
+        for q in range(*plan.spans[p]):
+            @pl.when(mz != q)
+            def _():
+                send(summed.at[pl.ds(q * slot, slot)], from_z.at[mz], (mx * nz + q, col), 12 + p)
+    for p in stages:
+        @pl.when(owner(p))
         def _():
-            send(piece(from_x.at[mx], q), from_z.at[mz], (mx * nz + q, col), 7)
-
-    @pl.when(mz < plan.owners)
-    def _():
-        from_z[mz] = from_x[mx, pl.ds(mz * slot, slot)]
-        wait_for(from_z.at[pl.ds(0, nz - 1)], recv_sem.at[7])
-        total = from_z[0]
-        for q in range(1, nz):
-            total = total + from_z[q]
-        gram_ref[strip, pl.ds(mx * plan.per_x + mz * slot, slot)] = total * (1.0 / plan.samples)
-        mine = gram_ref.at[strip, pl.ds(mx * plan.per_x + mz * slot, slot)]
-        for d in range(1, nz):
-            send(mine, mine, (mx * nz + lax.rem(mz + d, nz), col), 8)
-        if plan.owners > 1:
-            wait_for(gram_ref.at[strip, pl.ds(0, plan.per_x - slot)], recv_sem.at[8])
-
-    @pl.when(mz >= plan.owners)
-    def _():
-        other = gram_ref.at[strip, pl.ds(mx * plan.per_x, plan.per_x)]
-        wait_for(other, recv_sem.at[8])
-
-    mine = gram_ref.at[strip, pl.ds(mx * plan.per_x, plan.per_x)]
-    for d in range(1, nx):
-        send(mine, mine, (lax.rem(mx + d, nx) * nz + mz, col), 9)
-    wait_for(gram_ref.at[strip, pl.ds(0, plan.blocks - plan.per_x)], recv_sem.at[9])
-    mine = gram_ref.at[strip]
-    send(mine, mine, sibling, 11)
-    for d in range(1, ny):
-        send(mine, mine, (me, lax.rem(my + d, ny) * 2 + core), 10, y_sem.at[my])
-    for d in range(1, ny):
-        q = lax.rem(my + d, ny)
-        other = gram_ref.at[core * ny + q]
-        wait_for(other, y_sem.at[q])
-        send(other, other, sibling, 11)
+            from_z[mz] = summed[pl.ds(mz * slot, slot)]
+            wait_for(from_z.at[pl.ds(0, nz - 1)], recv_sem.at[12 + p])
+            total = from_z[0]
+            for q in range(1, nz):
+                total = total + from_z[q]
+            gram_ref[strip, pl.ds(mx * plan.per_x + mz * slot, slot)] = total * (1.0 / plan.samples)
+            mine = gram_ref.at[strip, pl.ds(mx * plan.per_x + mz * slot, slot)]
+            for d in range(1, nz):
+                send(mine, mine, (mx * nz + lax.rem(mz + d, nz), col), 15 + p)
+
+    def all_but_own(p, sem):
+        low, high = plan.spans[p]
+
+        @pl.when(owner(p))
+        def _():
+            if high - low > 1:
+                wait_for(summed.at[pl.ds(0, (high - low - 1) * slot)], sem)
+
+        @pl.when(jnp.logical_not(owner(p)))
+        def _():
+            wait_for(summed.at[pl.ds(0, (high - low) * slot)], sem)
+
+    for p in stages:
+        all_but_own(p, recv_sem.at[15 + p])
+        mine = gram_ref.at[strip, span(p, mx)]
+        for d in range(1, plane):
+            send(mine, mine, across(d)[2], 18 + p)
+    for p in stages:
+        wait_for(from_plane.at[pl.ds(0, plane - 1), span(p)], recv_sem.at[18 + p])
+        for x in range(nx):
+            mine = gram_ref.at[pl.ds(core * ny, ny), span(p, x)]
+            send(mine, mine, sibling, 5)
+
     def home(k, carry):
         device = peer(k)
         send(back.at[device], out_ref.at[me], (device, col), 2)
         return carry
 
     lax.fori_loop(1, n, home, 0)
-    wait_for(gram_ref.at[pl.ds(0, ny)], recv_sem.at[11])
+    wait_for(gram_ref.at[pl.ds(0, ny)], recv_sem.at[5])
 
     def block(k, c):
         return gram_ref[:, plan.pairs.index((k, c))].reshape(TILE, TILE)
@@ -338,20 +336,16 @@
     wait_for(out_ref.at[pl.ds(0, n - 1)], send_sem.at[2])
     wait_for(gathered.at[pl.ds(0, nc - 1)], send_sem.at[3])
     wait_for(from_core, send_sem.at[4])
-    @pl.when(mz < plan.owners)
-    def _():
-        if plan.owners > 1:
-            wait_for(from_x.at[0, pl.ds(0, (plan.owners - 1) * slot)], send_sem.at[7])
-        wait_for(from_z.at[pl.ds(0, nz - 1)], send_sem.at[8])
-
-    @pl.when(mz >= plan.owners)
-    def _():
-        wait_for(from_x.at[0], send_sem.at[7])
-
-    wait_for(gram_ref.at[strip, pl.ds(0, plan.blocks - plan.per_x)], send_sem.at[9])
-    if ny > 1:
-        wait_for(gram_ref.at[pl.ds(0, ny - 1)], send_sem.at[10])
-    wait_for(gram_ref.at[pl.ds(0, ny)], send_sem.at[11])
+    for p in stages:
+        wait_for(from_plane.at[pl.ds(0, plane - 1), span(p)], send_sem.at[9 + p])
+        all_but_own(p, send_sem.at[12 + p])
+
+        @pl.when(owner(p))
+        def _():
+            wait_for(from_z.at[pl.ds(0, nz - 1)], send_sem.at[15 + p])
+
+        wait_for(from_plane.at[pl.ds(0, plane - 1), span(p)], send_sem.at[18 + p])
+    wait_for(gram_ref.at[pl.ds(0, ny)], send_sem.at[5])
 
 
 def per_device(nx, nz, nc, slab_rows, row_flips, sample_holder, sample_offset):
@@ -361,9 +355,6 @@
     n, ny, chunk, strip = plan.n, plan.ny, plan.chunk, plan.strip
     rows = n // nc * chunk
     vmem = pl.BlockSpec(memory_space=pltpu.VMEM)
-    signs = (1 - 2 * row_flips).astype(F32).reshape(local // TILE, TILE)
-    key = (sample_holder[:, 0] * local + sample_offset).reshape(1, per_owner)
-
     def buffer(*shape, dtype=F32):
         return pltpu.VMEM(shape, dtype)
 
@@ -373,7 +364,7 @@
             jax.ShapeDtypeStruct((n, chunk, width), F32),
             jax.ShapeDtypeStruct((nc * TILE, width), F32),
         ),
-        in_specs=[vmem] * 3,
+        in_specs=[vmem] * 4,
         out_specs=(vmem, vmem),
         scratch_shapes=[
             buffer(n, 1, per_owner, dtype=jnp.int32),
@@ -388,16 +379,15 @@
             buffer(nc, plan.blocks, strip, TILE),
             buffer(ny, plan.blocks, strip, TILE),
             buffer(ny, plan.blocks, strip, TILE),
-            buffer(ny, plan.blocks, strip, TILE),
-            buffer(nx, plan.per_x, strip, TILE),
+            buffer(nx * ny, plan.per_x, strip, TILE),
+            buffer(plan.per_x, strip, TILE),
             buffer(nz, plan.per_z, strip, TILE),
-            pltpu.SemaphoreType.DMA((12,)),
-            pltpu.SemaphoreType.DMA((12,)),
-            pltpu.SemaphoreType.DMA((ny,)),
+            pltpu.SemaphoreType.DMA((21,)),
+            pltpu.SemaphoreType.DMA((21,)),
         ],
         compiler_params=pltpu.CompilerParams(collective_id=0, has_side_effects=True, vmem_limit_bytes=48 * 2**20),
         name="mix",
-    )(slab_rows, signs, key)
+    )(slab_rows, row_flips.reshape(local // TILE, TILE), sample_holder.reshape(1, per_owner), sample_offset.reshape(1, per_owner))
 
     return (mixed.reshape(local, width), precond)
 

time: 200 us -> 182 us (0.910)
  the two profiles are of different devices: /device:TPU:1 before, /device:TPU:8 now
where the time goes in v5:
time: 182 us
  Pallas kernels  177 us (97%)
  local copies, waits for them, and re-layouts  4.34 us (2%)
    pallas_call x1, Pallas kernels, per_device(): pl.pallas_call(functools.partial(mix_kernel, plan), out_shape=(jax.ShapeD...  177 us
    unnamed x10, local copies, waits for them, and re-layouts  4.34 us

profile of v5, /device:TPU:8, one launch (start us, length us, event | category | flops | bytes accessed | tf_op | source)
XLA Modules:
  0.0 181.9 jit_solution(7824705015558000535)
XLA Ops:
  0.6 0.0 copy-start.2
  0.6 0.0 copy-start.3
  0.7 0.6 copy-done.2
  1.3 0.0 copy-done.3
  1.3 0.0 copy-start
  1.3 1.2 copy-done
  2.5 0.0 copy-start.1
  2.5 0.7 copy-done.1
  3.2 176.9 %mix.1 = (f32[64,32,128]{2,1,0:T(8,128)S(1)}, f32[1024,128]{1,0:T(8,128)S(1)}) custom-call(f32[2048,128]{1,0:T(8,128)S(1)} %copy-done, s32[16,128]{1,0:T(8,128)S(1)} %bitcast.5, s32[1,128]{1,0:T(1,128)S(1)} %bitcast.6, s32[1,128]{1,0:T(1,128)S(1)} %bitcast.7), custom_call_target="tpu_custom_call" | custom-call | tf_op jit(solution)/shard_map/mix/pallas_call | solution.py:361
  180.1 1.0 copy.8
  181.1 0.8 copy.9
Async XLA Ops:
  0.6 0.7 copy-start.2
  0.6 0.7 copy-start.3
  1.3 1.2 copy-start
  2.5 0.7 copy-start.1

commit v6 on v5

--- a/solution.py
+++ b/solution.py
@@ -185,11 +185,19 @@
     def there(k, carry):
         device = (peer(k), col)
         send(keys_ref.at[me], keys_ref.at[me], device, 0)
-        send(work.at[device[0]], recv.at[me], device, 1)
+        return carry
+
+    half = plan.chunk // 2
+
+    def there_half(k, carry, h):
+        device = peer(k)
+        send(work.at[device, pl.ds(h * half, half)], recv.at[me, pl.ds(h * half, half)], (device, col), 1 if h == 0 else 7)
         return carry
 
     keys_ref[me] = holder_ref[...] * local + offset_ref[...]
     lax.fori_loop(1, n, there, 0)
+    for h in range(2):
+        lax.fori_loop(1, n, functools.partial(there_half, h=h), 0)
     recv[me] = work[me]
 
     per_col = n // nc
@@ -205,31 +213,40 @@
         return total + jnp.where(bins == where, 1.0, 0.0)
 
     counts = jnp.sum(lax.fori_loop(0, n, count, jnp.zeros((rows, TILE), F32)), axis=1, keepdims=True)
-    wait_for(recv.at[pl.ds(0, n - 1)], recv_sem.at[1])
     radix = min(8, n)
 
-    def low(g, carry):
-        mixed = butterfly([recv[radix * g + i] for i in range(radix)])
+    def low(g, carry, rows_of):
+        mixed = butterfly([recv[radix * g + i, rows_of] for i in range(radix)])
         for i in range(radix):
-            recv[radix * g + i] = mixed[i]
-        return carry
-
-    def high(i, carry):
-        mixed = butterfly([recv[radix * g + i] for g in range(n // radix)])
+            recv[radix * g + i, rows_of] = mixed[i]
+        return carry
+
+    def high(i, carry, rows_of):
+        mixed = butterfly([recv[radix * g + i, rows_of] for g in range(n // radix)])
         for g in range(n // radix):
-            back[radix * g + i] = mixed[g] * scale
-        return carry
-
-    lax.fori_loop(0, n // radix, low, 0)
-    lax.fori_loop(0, radix, high, 0)
-
-    for d in range(1, nc):
-        to = lax.rem(col + d, nc)
-        send(back.at[pl.ds(to * per_col, per_col)], gathered.at[col], (me, to), 3)
-
+            back[radix * g + i, rows_of] = mixed[g] * scale
+        return carry
+
+    for h in range(2):
+        rows_of = pl.ds(h * half, half)
+        wait_for(recv.at[pl.ds(0, n - 1), rows_of], recv_sem.at[1 if h == 0 else 7])
+        lax.fori_loop(0, n // radix, functools.partial(low, rows_of=rows_of), 0)
+        lax.fori_loop(0, radix, functools.partial(high, rows_of=rows_of), 0)
+        for d in range(1, nc):
+            to = lax.rem(col + d, nc)
+            send(back.at[pl.ds(to * per_col, per_col), rows_of], gathered.at[col, pl.ds(0, per_col), rows_of], (me, to), 3 if h == 0 else 8)
+
+    def home(k, carry):
+        device = peer(k)
+        send(back.at[device], out_ref.at[me], (device, col), 2)
+        return carry
+
+    early = n // 4
+    lax.fori_loop(n - early, n, home, 0)
     out_ref[me] = back[me]
     gathered[col] = back[pl.ds(col * per_col, per_col)]
-    wait_for(gathered.at[pl.ds(0, nc - 1)], recv_sem.at[3])
+    wait_for(gathered.at[pl.ds(0, nc - 1), pl.ds(0, per_col), pl.ds(0, half)], recv_sem.at[3])
+    wait_for(gathered.at[pl.ds(0, nc - 1), pl.ds(0, per_col), pl.ds(0, half)], recv_sem.at[8])
 
     for c in range(nc):
         here = gathered[c].reshape(rows, TILE)
@@ -317,12 +334,7 @@
             mine = gram_ref.at[pl.ds(core * ny, ny), span(p, x)]
             send(mine, mine, sibling, 5)
 
-    def home(k, carry):
-        device = peer(k)
-        send(back.at[device], out_ref.at[me], (device, col), 2)
-        return carry
-
-    lax.fori_loop(1, n, home, 0)
+    lax.fori_loop(1, n - early, home, 0)
     wait_for(gram_ref.at[pl.ds(0, ny)], recv_sem.at[5])
 
     def block(k, c):
@@ -332,9 +344,11 @@
 
     wait_for(out_ref.at[pl.ds(0, n - 1)], recv_sem.at[2])
     wait_for(keys_ref.at[pl.ds(0, n - 1)], send_sem.at[0])
-    wait_for(recv.at[pl.ds(0, n - 1)], send_sem.at[1])
+    wait_for(recv.at[pl.ds(0, n - 1), pl.ds(0, half)], send_sem.at[1])
+    wait_for(recv.at[pl.ds(0, n - 1), pl.ds(0, half)], send_sem.at[7])
     wait_for(out_ref.at[pl.ds(0, n - 1)], send_sem.at[2])
-    wait_for(gathered.at[pl.ds(0, nc - 1)], send_sem.at[3])
+    wait_for(gathered.at[pl.ds(0, nc - 1), pl.ds(0, per_col), pl.ds(0, half)], send_sem.at[3])
+    wait_for(gathered.at[pl.ds(0, nc - 1), pl.ds(0, per_col), pl.ds(0, half)], send_sem.at[8])
     wait_for(from_core, send_sem.at[4])
     for p in stages:
         wait_for(from_plane.at[pl.ds(0, plane - 1), span(p)], send_sem.at[9 + p])

time: 182 us -> 176 us (0.967)
  the two profiles are of different devices: /device:TPU:8 before, /device:TPU:1 now
where the time goes in v6:
time: 176 us; the launch traced here: 175 us
  Pallas kernels  170 us (97%)
  local copies, waits for them, and re-layouts  4.34 us (2%)
    pallas_call x1, Pallas kernels, per_device(): pl.pallas_call(functools.partial(mix_kernel, plan), out_shape=(jax.ShapeD...  170 us
    unnamed x10, local copies, waits for them, and re-layouts  4.34 us

profile of v6, /device:TPU:1, one launch (start us, length us, event | category | flops | bytes accessed | tf_op | source)
XLA Modules:
  0.0 175.3 jit_solution(15850248602558856536)
XLA Ops:
  0.6 0.0 copy-start.2
  0.6 0.0 copy-start.3
  0.7 0.6 copy-done.2
  1.3 0.0 copy-done.3
  1.3 0.0 copy-start
  1.3 1.2 copy-done
  2.5 0.0 copy-start.1
  2.5 0.7 copy-done.1
  3.2 170.3 %mix.1 = (f32[64,32,128]{2,1,0:T(8,128)S(1)}, f32[1024,128]{1,0:T(8,128)S(1)}) custom-call(f32[2048,128]{1,0:T(8,128)S(1)} %copy-done, s32[16,128]{1,0:T(8,128)S(1)} %bitcast.5, s32[1,128]{1,0:T(1,128)S(1)} %bitcast.6, s32[1,128]{1,0:T(1,128)S(1)} %bitcast.7), custom_call_target="tpu_custom_call" | custom-call | tf_op jit(solution)/shard_map/mix/pallas_call | solution.py:375
  173.5 1.0 copy.8
  174.5 0.8 copy.9
Async XLA Ops:
  0.6 0.7 copy-start.2
  0.6 0.7 copy-start.3
  1.3 1.2 copy-start
  2.5 0.7 copy-start.1
